TPU v7x, 256 devices: a whole 4x4x8 slice. The times are simulated.
256 devices in a mesh: gx: 16 (over y, x), gy: 8 (over z), gz: 2 (over core).
Axes of the slice: x: 4, y: 4, z: 8, core: 2. Of those that a mesh axis runs over, the one named last changes fastest.
Arguments:
- fine_field: bfloat16 [20480, 8, 8, 128], P(('gx', 'gy', 'gz')), may hold values from -6 to 6
- target: int32 [20480], P(('gx', 'gy', 'gz')), may hold values from 0 to 36863, as said below
- neighbour: int32 [4608, 6], P(('gx', 'gy', 'gz')), may hold values from -1 to 4607, as said below
- down_weight: bfloat16 [1024, 256], replicated, may hold values from -0.1875 to 0.1875
- conv_weight: bfloat16 [7, 256, 256], replicated, may hold values from -0.125 to 0.125
- out_cotangent: bfloat16 [4608, 4, 4, 4, 256], P(('gx', 'gy', 'gz')), may hold values from -6 to 6
Outputs:
- coarse_field: bfloat16 [4608, 4, 4, 4, 256], P(('gx', 'gy', 'gz'))
- fine_gradient: bfloat16 [20480, 8, 8, 128], P(('gx', 'gy', 'gz'))
- down_gradient: float32 [1024, 256], replicated
- conv_gradient: float32 [7, 256, 256], replicated
Inputs may be any that keep to these rules, and one draw needn't show every extreme that they name: `target`: no two fine bricks name the same octant. A fine brick names a coarse brick on its own device or on a device with the same gz index whose gx and gy indices each differ from its own by at most one. At most 20 of a device's fine bricks name a coarse brick on another device; at most 8 name one given other device, and every device sends exactly 8 to some device. `neighbour`: the relation is symmetric: if brick b names n across its +x face, n names b across its -x face (likewise for y and z). A named brick lies on the same device or on the adjacent device along that face's direction (no wrap). Across one face direction exactly 8 bricks of a device name bricks on the adjacent device where that device exists.
All inputs are finite; a program needn't handle non-finite values.
Results may differ from a plain program's by a relative error of at most 0.0061.
Values may be sent and summed in bfloat16 or wider, within the bound.
A program may use at most 128 MiB of HBM per device.

v0:
```python
import jax
import jax.numpy as jnp
from jax import lax
from jax.sharding import PartitionSpec as P

CAP = 8


opposite = (0, 2, 1, 4, 3, 6, 5)
offsets = ((-1, -1), (-1, 0), (-1, 1), (0, -1), (0, 1), (1, -1), (1, 0), (1, 1))


def from_behind(array, axis, by):
    count = lax.axis_size(axis)
    pairs = [(i, i + by) for i in range(count) if 0 <= i + by < count]
    return lax.ppermute(array, axis, pairs)


def to_grid(octants, blocks):
    channels = octants.shape[-1]
    spread = octants.reshape(blocks, 2, 2, 2, 2, 2, 2, channels)
    return spread.transpose(0, 1, 4, 2, 5, 3, 6, 7).reshape(blocks, 4, 4, 4, channels)


def from_grid(grid_field):
    blocks = grid_field.shape[0]
    channels = grid_field.shape[-1]
    spread = grid_field.reshape(blocks, 2, 2, 2, 2, 2, 2, channels)
    return spread.transpose(0, 1, 3, 5, 2, 4, 6, 7).reshape(blocks * 8, 8, channels)


def silu_slope(values):
    sigmoid_v = jax.nn.sigmoid(values)
    return sigmoid_v * (1.0 + values * (1.0 - sigmoid_v))


def flatten_rows(values):
    return values.reshape(-1, values.shape[-1])


def shifted_views(center, face_list):
    view_list = [center]
    for axis_pos in range(3):
        grid_dim = axis_pos + 1
        lower_face = jnp.expand_dims(face_list[2 * axis_pos], grid_dim)
        upper_face = jnp.expand_dims(face_list[2 * axis_pos + 1], grid_dim)
        inner_lower = lax.slice_in_dim(center, 0, 3, axis=grid_dim)
        inner_upper = lax.slice_in_dim(center, 1, 4, axis=grid_dim)
        view_list.append(jnp.concatenate([lower_face, inner_lower], axis=grid_dim))
        view_list.append(jnp.concatenate([inner_upper, upper_face], axis=grid_dim))
    return view_list


def collect_faces(field, neighbour, myself):
    blocks = field.shape[0]
    face_list = []
    for axis_pos in range(3):
        grid_dim = axis_pos + 1
        for side_index in range(2):
            column = neighbour[:, 2 * axis_pos + side_index]
            layer_at = 3 if side_index == 0 else 0
            offset = 1 if side_index == 0 else -1
            own_layer = lax.index_in_dim(field, layer_at, grid_dim, keepdims=False)
            safe_slot = jnp.where(column >= 0, column % blocks, 0)
            if axis_pos == 0:
                received = from_behind(own_layer, "gx", offset)
            elif axis_pos == 1:
                received = from_behind(own_layer, "gy", offset)
            else:
                received = from_behind(own_layer, "gz", offset)
            remote = received[safe_slot]
            local_face = own_layer[safe_slot]
            at_home = column // blocks == myself
            chosen = jnp.where(at_home[:, None, None, None], local_face, remote)
            face_list.append(
                jnp.where((column >= 0)[:, None, None, None], chosen, jnp.zeros_like(chosen))
            )
    return face_list


def shards(fine_field, target, neighbour, down_weight, conv_weight, out_cotangent):
    fine_count = fine_field.shape[0]
    blocks = neighbour.shape[0]
    cells_dev = blocks * 8
    channels = down_weight.shape[1]
    along_y = lax.axis_size("gy")
    z_depth = lax.axis_size("gz")
    myself = lax.axis_index(("gx", "gy")) * z_depth + lax.axis_index("gz")
    voxel_scale = 1.0 / (64 * blocks)
    slots_all = 8 * CAP
    fine_rows = fine_field.reshape(fine_count * 8, -1)
    reduced = jnp.dot(fine_rows, down_weight, preferred_element_type=jnp.float32).astype(
        jnp.bfloat16
    )
    reduced = reduced.reshape(fine_count, 8, channels)
    owner_dev = target // cells_dev
    cell_local = target % cells_dev
    moving = owner_dev != myself
    step_a = owner_dev // (along_y * z_depth) - lax.axis_index("gx")
    step_b = owner_dev // z_depth % along_y - lax.axis_index("gy")
    flat_dir = (step_a + 1) * 3 + (step_b + 1)
    dest_dir = jnp.where(flat_dir > 4, flat_dir - 1, flat_dir)
    member = (
        (dest_dir[:, None] == jnp.arange(8, dtype=jnp.int32)[None, :]) & moving[:, None]
    ).astype(jnp.int32)
    before = jnp.cumsum(member, axis=0) - member
    order_in = jnp.sum(before * member, axis=1)
    send_slot = jnp.where(moving, dest_dir * CAP + order_in, slots_all)
    outgoing = (
        jnp.zeros((slots_all, 8, channels), jnp.bfloat16).at[send_slot].set(reduced, mode="drop")
    )
    names_out = jnp.zeros((slots_all,), jnp.int32).at[send_slot].set(cell_local + 1, mode="drop")
    outgoing = outgoing.reshape(8, CAP, 8, channels)
    names_out = names_out.reshape(8, CAP)
    piece_list = []
    name_list = []
    for place, (step_x, step_y) in enumerate(offsets):
        piece, piece_names = from_behind(
            (outgoing[place], names_out[place]), ("gx", "gy"), step_x * along_y + step_y
        )
        piece_list.append(piece)
        name_list.append(piece_names)
    arrived = jnp.stack(piece_list)
    arrived_raw = jnp.stack(name_list)
    arrived = arrived.reshape(slots_all, 8, channels)
    arrived_names = jnp.where(arrived_raw > 0, arrived_raw - 1, -1).reshape(slots_all)
    octant_table = jnp.zeros((cells_dev, 8, channels), jnp.bfloat16)
    octant_table = octant_table.at[jnp.where(moving, cells_dev, cell_local)].set(
        reduced, mode="drop"
    )
    octant_table = octant_table.at[jnp.where(arrived_names >= 0, arrived_names, cells_dev)].set(
        arrived, mode="drop"
    )
    before_act = to_grid(octant_table, blocks)
    hidden = jax.nn.silu(before_act.astype(jnp.float32)).astype(jnp.bfloat16)
    hidden_views = shifted_views(hidden, collect_faces(hidden, neighbour, myself))
    summed = jnp.zeros((blocks * 64, channels), jnp.float32)
    for direction in range(7):
        summed = summed + jnp.dot(
            flatten_rows(hidden_views[direction]),
            conv_weight[direction],
            preferred_element_type=jnp.float32,
        )
    coarse_field = summed.astype(jnp.bfloat16).reshape(hidden.shape)
    grad_views = shifted_views(out_cotangent, collect_faces(out_cotangent, neighbour, myself))
    grad_rows = flatten_rows(out_cotangent)
    backward = jnp.zeros((blocks * 64, channels), jnp.float32)
    weight_terms = []
    for direction in range(7):
        backward = backward + lax.dot_general(
            flatten_rows(grad_views[opposite[direction]]),
            conv_weight[direction],
            (((1,), (1,)), ((), ())),
            preferred_element_type=jnp.float32,
        )
        weight_terms.append(
            lax.dot_general(
                flatten_rows(hidden_views[direction]),
                grad_rows,
                (((0,), (0,)), ((), ())),
                preferred_element_type=jnp.float32,
            )
        )
    conv_local = jnp.stack(weight_terms) * voxel_scale
    grad_before = (
        backward.reshape(before_act.shape) * silu_slope(before_act.astype(jnp.float32))
    ).astype(jnp.bfloat16)
    grad_cells = from_grid(grad_before)
    sending_back = jnp.where(
        (arrived_names >= 0)[:, None, None],
        grad_cells[jnp.maximum(arrived_names, 0)],
        jnp.zeros((slots_all, 8, channels), jnp.bfloat16),
    ).reshape(8, CAP, 8, channels)
    back_list = []
    for place, (step_x, step_y) in enumerate(offsets):
        back_list.append(
            from_behind(sending_back[place], ("gx", "gy"), -(step_x * along_y + step_y))
        )
    returned = jnp.stack(back_list)
    returned = returned.reshape(slots_all, 8, channels)
    grad_reduced = jnp.where(
        moving[:, None, None],
        returned[jnp.minimum(send_slot, slots_all - 1)],
        grad_cells[cell_local],
    )
    grad_reduced_rows = grad_reduced.reshape(fine_count * 8, channels)
    fine_gradient = (
        lax.dot_general(
            grad_reduced_rows,
            down_weight,
            (((1,), (1,)), ((), ())),
            preferred_element_type=jnp.float32,
        )
        .astype(jnp.bfloat16)
        .reshape(fine_field.shape)
    )
    down_local = (
        lax.dot_general(
            fine_rows,
            grad_reduced_rows,
            (((0,), (0,)), ((), ())),
            preferred_element_type=jnp.float32,
        )
        * voxel_scale
    )
    down_total, conv_total = lax.psum((down_local, conv_local), ("gx", "gy", "gz"))
    return (coarse_field, fine_gradient, down_total, conv_total)


def solution(mesh):
    in_specs = (
        P(("gx", "gy", "gz"), None, None, None),
        P(("gx", "gy", "gz")),
        P(("gx", "gy", "gz"), None),
        P(),
        P(),
        P(("gx", "gy", "gz"), None, None, None, None),
    )
    out_specs = (
        P(("gx", "gy", "gz"), None, None, None, None),
        P(("gx", "gy", "gz"), None, None, None),
        P(),
        P(),
    )
    return jax.shard_map(shards, mesh=mesh, in_specs=in_specs, out_specs=out_specs, check_vma=False)
```

profile of v0, /device:TPU:1, one launch (start us, length us, event | category | flops | bytes accessed | tf_op | source)
XLA Modules:
  0.0 695.3 jit_solution(10016535410411485566)
XLA Ops:
  9.4 5.3 collective-permute-start.7
  16.5 3.8 collective-permute-start.23
  23.3 4.2 collective-permute-start.25
  61.1 4.0 collective-permute-start.6
  65.8 6.3 collective-permute-start.5
  80.5 8.6 %collective-permute-done.2 = s32[8]{0:T(128)S(1)} collective-permute-done((s32[8]{0:T(128)S(1)}, s32[8]{0:T(128)S(1)}, u32[]{:S(2)}, u32[]{:S(2)}) %collective-permute-start.2) | collective-permute-done | bytes 64 | tf_op jit(solution)/shard_map/ppermute | solution.py:16
  94.9 3.9 collective-permute-done
  100.8 5.7 collective-permute-done.8
  107.8 5.5 collective-permute-done.9
  114.5 9.6 %collective-permute-done.10 = bf16[8,8,256]{2,1,0:T(8,128)(2,1)S(1)} collective-permute-done((bf16[8,8,256]{2,1,0:T(8,128)(2,1)S(1)}, bf16[8,8,256]{2,1,0:T(8,128)(2,1)S(1)}, u32[]{:S(2)}, u32[]{:S(2)}) %collective-permute-start.10) | collective-permute-done | bytes 32800 | tf_op jit(solution)/shard_map/ppermute | solution.py:16
  125.4 3.3 collective-permute-done.11
  131.4 10.8 %collective-permute-start.13 = (bf16[8,8,256]{2,1,0:T(8,128)(2,1)S(1)}, bf16[8,8,256]{2,1,0:T(8,128)(2,1)S(1)}, u32[]{:S(2)}, u32[]{:S(2)}) collective-permute-start(bf16[8,8,256]{2,1,0:T(8,128)(2,1)S(1)} %get-tuple-element.62), channel_id=1, source_target_pairs={{0,14},{2,16},{4,18},{6,20},{8,22},{10,24},{12,26},{14,28},{16,30}... | collective-permute-start | bytes 98312 | tf_op jit(solution)/shard_map/ppermute | solution.py:16
  143.2 5.7 collective-permute-start.14
  150.0 7.3 %collective-permute-start.15 = (bf16[8,8,256]{2,1,0:T(8,128)(2,1)S(1)}, bf16[8,8,256]{2,1,0:T(8,128)(2,1)S(1)}, u32[]{:S(2)}, u32[]{:S(2)}) collective-permute-start(bf16[8,8,256]{2,1,0:T(8,128)(2,1)S(1)} %get-tuple-element.60), channel_id=1, source_target_pairs={{0,18},{2,20},{4,22},{6,24},{8,26},{10,28},{12,30},{14,32},{16,34}... | collective-permute-start | bytes 98312 | tf_op jit(solution)/shard_map/ppermute | solution.py:16
  158.3 19.9 %collective-permute-start.26 = (bf16[18,4,4,256]{3,2,1,0:T(4,128)(2,1)}, bf16[18,4,4,256]{3,2,1,0:T(4,128)(2,1)}, u32[]{:S(2)}, u32[]{:S(2)}) collective-permute-start(bf16[18,4,4,256]{3,2,1,0:T(4,128)(2,1)} %bitcast.370), channel_id=1, source_target_pairs={{1,0},{3,2},{5,4},{7,6},{9,8},{11,10},{13,12},{15,14},{17,16},{19,... | collective-permute-start | bytes 442376 | tf_op jit(solution)/shard_map/ppermute | solution.py:16
  209.3 12.2 %collective-permute-start.27 = (bf16[18,4,4,256]{3,2,1,0:T(4,128)(2,1)}, bf16[18,4,4,256]{3,2,1,0:T(4,128)(2,1)}, u32[]{:S(2)}, u32[]{:S(2)}) collective-permute-start(bf16[18,4,4,256]{3,2,1,0:T(4,128)(2,1)} %bitcast.369), channel_id=1, source_target_pairs={{0,1},{2,3},{4,5},{6,7},{8,9},{10,11},{12,13},{14,15},{16,17},{18,... | collective-permute-start | bytes 442376 | tf_op jit(solution)/shard_map/ppermute | solution.py:16
  221.5 4.1 collective-permute-start.21
  237.9 11.5 %collective-permute-start.16 = (bf16[18,4,4,256]{3,0,2,1:T(8,128)(2,1)S(1)}, bf16[18,4,4,256]{3,0,2,1:T(8,128)(2,1)}, u32[]{:S(2)}, u32[]{:S(2)}) collective-permute-start(bf16[18,4,4,256]{3,0,2,1:T(8,128)(2,1)S(1)} %get-tuple-element.39), channel_id=1, source_target_pairs={{0,16},{16,32},{32,48},{48,64},{64,80},{80,96},{96,112},{112,128},... | collective-permute-start | bytes 442376 | tf_op jit(solution)/shard_map/ppermute | solution.py:16
  255.2 4.7 collective-permute-start.18
  318.4 4.0 collective-permute-start.28
  364.7 14.7 %collective-permute-start.29 = (bf16[8,8,256]{2,1,0:T(8,128)(2,1)}, bf16[8,8,256]{2,1,0:T(8,128)(2,1)S(1)}, u32[]{:S(2)}, u32[]{:S(2)}) collective-permute-start(bf16[8,8,256]{2,1,0:T(8,128)(2,1)} %get-tuple-element.58), channel_id=1, source_target_pairs={{0,16},{2,18},{4,20},{6,22},{8,24},{10,26},{12,28},{14,30},{16,32}... | collective-permute-start | bytes 98312 | tf_op jit(solution)/shard_map/ppermute | solution.py:16
  380.7 5.8 collective-permute-start.30
  387.9 4.2 collective-permute-start.31
  415.6 268.6 %all-reduce.3.cloned.1.call-done = (f32[1024,256]{0,1:T(8,128)}, f32[7,256,256]{2,1,0:T(8,128)}) async-done(((f32[1024,256]{0,1:T(8,128)}, f32[7,256,256]{2,1,0:T(8,128)}), (f32[1024,256]{0,1:T(8,128)}, f32[7,256,256]{2,1,0:T(8,128)})) %all-reduce.3.cloned.1.call-update) | async-done | bytes 2883600 | tf_op jit(solution)/shard_map/psum | solution.py:206
  (349 shorter events, 246.0 us)
Async XLA Ops:
  7.2 677.0 %all-reduce.3.cloned.1.call-start = ((), (), s32[]{:S(2)}) async-start(), calls=%async_computation | async-start | bytes 5767168 | tf_op jit(solution)/shard_map/psum | solution.py:206
  9.4 51.7 %collective-permute-start.7 = (s32[8]{0:T(128)S(1)}, s32[8]{0:T(128)S(1)}, u32[]{:S(2)}, u32[]{:S(2)}) collective-permute-start(s32[8]{0:T(128)S(1)} %get-tuple-element.100), channel_id=1, source_target_pairs={{0,18},{2,20},{4,22},{6,24},{8,26},{10,28},{12,30},{14,32},{16,34}... | collective-permute-start | bytes 104 | tf_op jit(solution)/shard_map/ppermute | solution.py:16
  16.5 192.8 %collective-permute-start.23 = (bf16[18,4,4,256]{3,2,1,0:T(4,128)(2,1)}, bf16[18,4,4,256]{3,2,1,0:T(4,128)(2,1)}, u32[]{:S(2)}, u32[]{:S(2)}) collective-permute-start(bf16[18,4,4,256]{3,2,1,0:T(4,128)(2,1)} %get-tuple-element.48), channel_id=1, source_target_pairs={{0,16},{16,32},{32,48},{48,64},{64,80},{80,96},{96,112},{112,128},... | collective-permute-start | bytes 442376 | tf_op jit(solution)/shard_map/ppermute | solution.py:16
  20.2 201.3 %collective-permute-start.22 = (bf16[18,4,4,256]{3,2,1,0:T(4,128)(2,1)}, bf16[18,4,4,256]{3,2,1,0:T(4,128)(2,1)}, u32[]{:S(2)}, u32[]{:S(2)}) collective-permute-start(bf16[18,4,4,256]{3,2,1,0:T(4,128)(2,1)} %get-tuple-element.49), channel_id=1, source_target_pairs={{16,0},{32,16},{48,32},{64,48},{80,64},{96,80},{112,96},{128,112},... | collective-permute-start | bytes 442376 | tf_op jit(solution)/shard_map/ppermute | solution.py:16
  23.3 202.3 %collective-permute-start.25 = (bf16[18,4,4,256]{3,2,1,0:T(4,128)(2,1)}, bf16[18,4,4,256]{3,2,1,0:T(4,128)(2,1)}, u32[]{:S(2)}, u32[]{:S(2)}) collective-permute-start(bf16[18,4,4,256]{3,2,1,0:T(4,128)(2,1)} %get-tuple-element.44), channel_id=1, source_target_pairs={{0,2},{2,4},{4,6},{6,8},{8,10},{10,12},{12,14},{1,3},{3,5},{5,7},{... | collective-permute-start | bytes 442376 | tf_op jit(solution)/shard_map/ppermute | solution.py:16
  27.6 206.7 %collective-permute-start.24 = (bf16[18,4,4,256]{3,2,1,0:T(4,128)(2,1)}, bf16[18,4,4,256]{3,2,1,0:T(4,128)(2,1)}, u32[]{:S(2)}, u32[]{:S(2)}) collective-permute-start(bf16[18,4,4,256]{3,2,1,0:T(4,128)(2,1)} %get-tuple-element.45), channel_id=1, source_target_pairs={{2,0},{4,2},{6,4},{8,6},{10,8},{12,10},{14,12},{3,1},{5,3},{7,5},{... | collective-permute-start | bytes 442376 | tf_op jit(solution)/shard_map/ppermute | solution.py:16
  79.2 9.9 %collective-permute-start.2 = (s32[8]{0:T(128)S(1)}, s32[8]{0:T(128)S(1)}, u32[]{:S(2)}, u32[]{:S(2)}) collective-permute-start(s32[8]{0:T(128)S(1)} %get-tuple-element.105), channel_id=1, source_target_pairs={{14,0},{16,2},{18,4},{20,6},{22,8},{24,10},{26,12},{28,14},{30,16}... | collective-permute-start | bytes 104 | tf_op jit(solution)/shard_map/ppermute | solution.py:16
  113.2 10.9 %collective-permute-start.10 = (bf16[8,8,256]{2,1,0:T(8,128)(2,1)S(1)}, bf16[8,8,256]{2,1,0:T(8,128)(2,1)S(1)}, u32[]{:S(2)}, u32[]{:S(2)}) collective-permute-start(bf16[8,8,256]{2,1,0:T(8,128)(2,1)S(1)} %get-tuple-element.65), channel_id=1, source_target_pairs={{14,0},{16,2},{18,4},{20,6},{22,8},{24,10},{26,12},{28,14},{30,16}... | collective-permute-start | bytes 98312 | tf_op jit(solution)/shard_map/ppermute | solution.py:16
  131.4 11.8 %collective-permute-start.13 = (bf16[8,8,256]{2,1,0:T(8,128)(2,1)S(1)}, bf16[8,8,256]{2,1,0:T(8,128)(2,1)S(1)}, u32[]{:S(2)}, u32[]{:S(2)}) collective-permute-start(bf16[8,8,256]{2,1,0:T(8,128)(2,1)S(1)} %get-tuple-element.62), channel_id=1, source_target_pairs={{0,14},{2,16},{4,18},{6,20},{8,22},{10,24},{12,26},{14,28},{16,30}... | collective-permute-start | bytes 98312 | tf_op jit(solution)/shard_map/ppermute | solution.py:16
  150.0 8.3 %collective-permute-start.15 = (bf16[8,8,256]{2,1,0:T(8,128)(2,1)S(1)}, bf16[8,8,256]{2,1,0:T(8,128)(2,1)S(1)}, u32[]{:S(2)}, u32[]{:S(2)}) collective-permute-start(bf16[8,8,256]{2,1,0:T(8,128)(2,1)S(1)} %get-tuple-element.60), channel_id=1, source_target_pairs={{0,18},{2,20},{4,22},{6,24},{8,26},{10,28},{12,30},{14,32},{16,34}... | collective-permute-start | bytes 98312 | tf_op jit(solution)/shard_map/ppermute | solution.py:16
  158.3 79.6 %collective-permute-start.26 = (bf16[18,4,4,256]{3,2,1,0:T(4,128)(2,1)}, bf16[18,4,4,256]{3,2,1,0:T(4,128)(2,1)}, u32[]{:S(2)}, u32[]{:S(2)}) collective-permute-start(bf16[18,4,4,256]{3,2,1,0:T(4,128)(2,1)} %bitcast.370), channel_id=1, source_target_pairs={{1,0},{3,2},{5,4},{7,6},{9,8},{11,10},{13,12},{15,14},{17,16},{19,... | collective-permute-start | bytes 442376 | tf_op jit(solution)/shard_map/ppermute | solution.py:16
  209.3 42.4 %collective-permute-start.27 = (bf16[18,4,4,256]{3,2,1,0:T(4,128)(2,1)}, bf16[18,4,4,256]{3,2,1,0:T(4,128)(2,1)}, u32[]{:S(2)}, u32[]{:S(2)}) collective-permute-start(bf16[18,4,4,256]{3,2,1,0:T(4,128)(2,1)} %bitcast.369), channel_id=1, source_target_pairs={{0,1},{2,3},{4,5},{6,7},{8,9},{10,11},{12,13},{14,15},{16,17},{18,... | collective-permute-start | bytes 442376 | tf_op jit(solution)/shard_map/ppermute | solution.py:16
  221.5 33.7 %collective-permute-start.21 = (bf16[18,4,4,256]{3,0,2,1:T(8,128)(2,1)}, bf16[18,4,4,256]{3,0,2,1:T(8,128)(2,1)}, u32[]{:S(2)}, u32[]{:S(2)}) collective-permute-start(bf16[18,4,4,256]{3,0,2,1:T(8,128)(2,1)} %get-tuple-element.30), channel_id=1, source_target_pairs={{1,0},{3,2},{5,4},{7,6},{9,8},{11,10},{13,12},{15,14},{17,16},{19,... | collective-permute-start | bytes 442376 | tf_op jit(solution)/shard_map/ppermute | solution.py:16
  225.7 38.1 %collective-permute-start.20 = (bf16[18,4,4,256]{3,0,2,1:T(8,128)(2,1)}, bf16[18,4,4,256]{3,0,2,1:T(8,128)(2,1)}, u32[]{:S(2)}, u32[]{:S(2)}) collective-permute-start(bf16[18,4,4,256]{3,0,2,1:T(8,128)(2,1)} %get-tuple-element.31), channel_id=1, source_target_pairs={{0,1},{2,3},{4,5},{6,7},{8,9},{10,11},{12,13},{14,15},{16,17},{18,... | collective-permute-start | bytes 442376 | tf_op jit(solution)/shard_map/ppermute | solution.py:16
  234.3 37.7 %collective-permute-start.17 = (bf16[18,4,4,256]{3,0,2,1:T(8,128)(2,1)S(1)}, bf16[18,4,4,256]{3,0,2,1:T(8,128)(2,1)}, u32[]{:S(2)}, u32[]{:S(2)}) collective-permute-start(bf16[18,4,4,256]{3,0,2,1:T(8,128)(2,1)S(1)} %get-tuple-element.38), channel_id=1, source_target_pairs={{16,0},{32,16},{48,32},{64,48},{80,64},{96,80},{112,96},{128,112},... | collective-permute-start | bytes 442376 | tf_op jit(solution)/shard_map/ppermute | solution.py:16
  237.9 37.4 %collective-permute-start.16 = (bf16[18,4,4,256]{3,0,2,1:T(8,128)(2,1)S(1)}, bf16[18,4,4,256]{3,0,2,1:T(8,128)(2,1)}, u32[]{:S(2)}, u32[]{:S(2)}) collective-permute-start(bf16[18,4,4,256]{3,0,2,1:T(8,128)(2,1)S(1)} %get-tuple-element.39), channel_id=1, source_target_pairs={{0,16},{16,32},{32,48},{48,64},{64,80},{80,96},{96,112},{112,128},... | collective-permute-start | bytes 442376 | tf_op jit(solution)/shard_map/ppermute | solution.py:16
  251.6 37.7 %collective-permute-start.19 = (bf16[18,4,4,256]{3,0,2,1:T(8,128)(2,1)}, bf16[18,4,4,256]{3,0,2,1:T(8,128)(2,1)}, u32[]{:S(2)}, u32[]{:S(2)}) collective-permute-start(bf16[18,4,4,256]{3,0,2,1:T(8,128)(2,1)} %get-tuple-element.34), channel_id=1, source_target_pairs={{2,0},{4,2},{6,4},{8,6},{10,8},{12,10},{14,12},{3,1},{5,3},{7,5},{... | collective-permute-start | bytes 442376 | tf_op jit(solution)/shard_map/ppermute | solution.py:16
  255.2 36.5 %collective-permute-start.18 = (bf16[18,4,4,256]{3,0,2,1:T(8,128)(2,1)}, bf16[18,4,4,256]{3,0,2,1:T(8,128)(2,1)}, u32[]{:S(2)}, u32[]{:S(2)}) collective-permute-start(bf16[18,4,4,256]{3,0,2,1:T(8,128)(2,1)} %get-tuple-element.35), channel_id=1, source_target_pairs={{0,2},{2,4},{4,6},{6,8},{8,10},{10,12},{12,14},{1,3},{3,5},{5,7},{... | collective-permute-start | bytes 442376 | tf_op jit(solution)/shard_map/ppermute | solution.py:16
  318.4 46.3 %collective-permute-start.28 = (bf16[8,8,256]{2,1,0:T(8,128)(2,1)}, bf16[8,8,256]{2,1,0:T(8,128)(2,1)}, u32[]{:S(2)}, u32[]{:S(2)}) collective-permute-start(bf16[8,8,256]{2,1,0:T(8,128)(2,1)} %get-tuple-element.59), channel_id=1, source_target_pairs={{0,18},{2,20},{4,22},{6,24},{8,26},{10,28},{12,30},{14,32},{16,34}... | collective-permute-start | bytes 98312 | tf_op jit(solution)/shard_map/ppermute | solution.py:16
  351.0 47.2 %collective-permute-start.35 = (bf16[8,8,256]{2,1,0:T(8,128)(2,1)}, bf16[8,8,256]{2,1,0:T(8,128)(2,1)}, u32[]{:S(2)}, u32[]{:S(2)}) collective-permute-start(bf16[8,8,256]{2,1,0:T(8,128)(2,1)} %get-tuple-element.52), channel_id=1, source_target_pairs={{18,0},{20,2},{22,4},{24,6},{26,8},{28,10},{30,12},{32,14},{34,16}... | collective-permute-start | bytes 98312 | tf_op jit(solution)/shard_map/ppermute | solution.py:16
  352.3 44.5 %collective-permute-start.34 = (bf16[8,8,256]{2,1,0:T(8,128)(2,1)}, bf16[8,8,256]{2,1,0:T(8,128)(2,1)}, u32[]{:S(2)}, u32[]{:S(2)}) collective-permute-start(bf16[8,8,256]{2,1,0:T(8,128)(2,1)} %get-tuple-element.53), channel_id=1, source_target_pairs={{16,0},{18,2},{20,4},{22,6},{24,8},{26,10},{28,12},{30,14},{32,16}... | collective-permute-start | bytes 98312 | tf_op jit(solution)/shard_map/ppermute | solution.py:16
  353.6 41.8 %collective-permute-start.33 = (bf16[8,8,256]{2,1,0:T(8,128)(2,1)}, bf16[8,8,256]{2,1,0:T(8,128)(2,1)}, u32[]{:S(2)}, u32[]{:S(2)}) collective-permute-start(bf16[8,8,256]{2,1,0:T(8,128)(2,1)} %get-tuple-element.54), channel_id=1, source_target_pairs={{14,0},{16,2},{18,4},{20,6},{22,8},{24,10},{26,12},{28,14},{30,16}... | collective-permute-start | bytes 98312 | tf_op jit(solution)/shard_map/ppermute | solution.py:16
  354.9 39.2 %collective-permute-start.32 = (bf16[8,8,256]{2,1,0:T(8,128)(2,1)}, bf16[8,8,256]{2,1,0:T(8,128)(2,1)}, u32[]{:S(2)}, u32[]{:S(2)}) collective-permute-start(bf16[8,8,256]{2,1,0:T(8,128)(2,1)} %get-tuple-element.55), channel_id=1, source_target_pairs={{2,0},{4,2},{6,4},{8,6},{10,8},{12,10},{14,12},{16,14},{18,16},{20... | collective-permute-start | bytes 98312 | tf_op jit(solution)/shard_map/ppermute | solution.py:16
  364.7 16.1 %collective-permute-start.29 = (bf16[8,8,256]{2,1,0:T(8,128)(2,1)}, bf16[8,8,256]{2,1,0:T(8,128)(2,1)S(1)}, u32[]{:S(2)}, u32[]{:S(2)}) collective-permute-start(bf16[8,8,256]{2,1,0:T(8,128)(2,1)} %get-tuple-element.58), channel_id=1, source_target_pairs={{0,16},{2,18},{4,20},{6,22},{8,24},{10,26},{12,28},{14,30},{16,32}... | collective-permute-start | bytes 98312 | tf_op jit(solution)/shard_map/ppermute | solution.py:16
  (71 other events, 452.7 us)
Sparse Core Ops, SparseCore 0:
  405.1 279.0 all-reduce.2
where the time goes:
time: 708 us; the launch traced here: 695 us
  waiting for transfers between devices  319 us (45%)
  local copies, waits for them, and re-layouts  153 us (22%)
  starting transfers between devices  153 us (22%)
  matrix products  27.3 us (4%)
  other arithmetic  26.7 us (4%)
  between operations  15.6 us (2%)
    psum x1, waiting for transfers between devices, shards(): lax.psum((down_local, conv_local), ('gx', 'gy', 'gz'))  269 us
    ppermute x36, starting transfers between devices, from_behind(): return lax.ppermute(array, axis, pairs)  153 us
    ppermute x36, waiting for transfers between devices, from_behind(): return lax.ppermute(array, axis, pairs)  50.5 us
    gather x12, local copies, waits for them, and re-layouts, collect_faces(): local_face = own_layer[safe_slot]  27.2 us
    gather x12, local copies, waits for them, and re-layouts, collect_faces(): remote = received[safe_slot]  23.3 us
    unnamed x135, local copies, waits for them, and re-layouts  19.4 us
    reshape x13, local copies, waits for them, and re-layouts, flatten_rows(): return values.reshape(-1, values.shape[-1])  18.3 us
  transfers between devices with their start and end apart: 37, of which 18 were waited for; matrix products, arithmetic and copies ran while one was open for 24% of the time, Pallas kernels for 0%

commit v1 on v0

v1 whole, which is shorter than its diff:
```python
import functools

import jax
import jax.numpy as jnp
from jax import lax
from jax.experimental import pallas as pl
from jax.experimental.pallas import tpu as pltpu
from jax.sharding import PartitionSpec as P

MESH = pl.DeviceIdType.MESH
BF = jnp.bfloat16
F32 = jnp.float32
I32 = jnp.int32

NX, NY, NZ = 16, 8, 2
MB = 18
BP = 32
NB = 80
CELLS = 8 * MB

OPP = (0, 2, 1, 4, 3, 6, 5)
OFFS = ((0, 0, 0), (-1, 0, 0), (1, 0, 0), (0, -1, 0), (0, 1, 0), (0, 0, -1), (0, 0, 1))
DIRS = ((-1, -1), (-1, 0), (-1, 1), (0, -1), (0, 1), (1, -1), (1, 0), (1, 1))
KA, KD = 112, 64


def iota(shape, dim):
    return lax.broadcasted_iota(I32, shape, dim)


def dot(a, b):
    return jnp.dot(a, b, preferred_element_type=F32)


def dot_nt(a, b):
    return lax.dot_general(a, b, (((1,), (1,)), ((), ())), preferred_element_type=F32)


def onehot(mask):
    return jnp.where(mask, 1.0, 0.0).astype(BF)


def ninth(u):
    return lax.shift_right_arithmetic(u * 7282, 16)


def view(ext, x, d):
    dx, dy, dz = OFFS[d]
    rows = ext[1 + x + dx, 1 + dy:5 + dy, BP * (1 + dz):BP * (5 + dz), :]
    return rows.reshape(16 * BP, 256)


def layer_quad(ext, k, q):
    if k == 0:
        return ext[4, 1 + q, BP:5 * BP, :]
    if k == 1:
        return ext[1, 1 + q, BP:5 * BP, :]
    if k == 2:
        return ext[1 + q, 4, BP:5 * BP, :]
    if k == 3:
        return ext[1 + q, 1, BP:5 * BP, :]
    z = 4 if k == 4 else 1
    return ext[1 + q, 1:5, BP * z:BP * (z + 1), :].reshape(4 * BP, 256)


def put_halo(ext, k, q, rows):
    if k == 0:
        ext[0, 1 + q, BP:5 * BP, :] = rows
    elif k == 1:
        ext[5, 1 + q, BP:5 * BP, :] = rows
    elif k == 2:
        ext[1 + q, 0, BP:5 * BP, :] = rows
    elif k == 3:
        ext[1 + q, 5, BP:5 * BP, :] = rows
    else:
        z = 0 if k == 4 else 5
        ext[1 + q, 1:5, BP * z:BP * (z + 1), :] = rows.reshape(4, BP, 256)


def kernel(fine, tgtc, tgtr, nbc, nbr, wd, wc, cot,
           coarse_o, fineg_o, ga, gd,
           cotx, hidx, gh, red, fine_t, hid_t, gbuf, gr, selc, selp,
           osnd, orcv, rsnd, rrcv, fsnd, frcv, hsnd, hrcv,
           pa, pd, ca, cd, qa, qd, xa, xd, za, zd, ya, yd, wa, wdn,
           csem, osem, rsem, fsem, hsem, coresem, xsem, zsem, zgsem, xgsem, cgsem):
    gx, gy, gz = lax.axis_index("gx"), lax.axis_index("gy"), lax.axis_index("gz")
    myself = (gx * NY + gy) * NZ + gz

    def at(dx, dy):
        return (lax.rem(gx + dx + NX, NX), lax.rem(gy + dy + NY, NY), gz)

    other = (gx, gy, 1 - gz)

    barrier = pltpu.get_barrier_semaphore()
    peers = [at(k, 0) for k in range(1, NX)] + [at(0, k) for k in range(1, NY)]
    peers += [at(a, b) for a in (-1, 1) for b in (-1, 1)] + [other]
    for peer in peers:
        pl.semaphore_signal(barrier, inc=1, device_id=peer, device_id_type=MESH)

    cot_in = pltpu.make_async_copy(cot, cotx.at[1:5, 1:5, BP:5 * BP, :], csem)
    cot_in.start()

    def remote(src, dst, sems, i, device):
        return pltpu.make_async_remote_copy(
            src_ref=src, dst_ref=dst, send_sem=sems.at[0, i], recv_sem=sems.at[1, i],
            device_id=device, device_id_type=MESH)

    def place(t):
        owner = ninth(lax.shift_right_arithmetic(t, 4))
        cell = t - owner * CELLS
        moving = owner != myself
        sx = lax.shift_right_arithmetic(owner, 4) - gx
        sy = (lax.shift_right_arithmetic(owner, 1) & 7) - gy
        flat = (sx + 1) * 3 + (sy + 1)
        return cell, moving, jnp.where(flat > 4, flat - 1, flat)

    cell_c, moving_c, dest_c = place(tgtc[...])
    cell_r, moving_r, dest_r = place(tgtr[...])
    member_c = jnp.where(moving_c & (dest_c == iota((NB, 128), 1)), 1.0, 0.0)
    lower = onehot(iota((NB, NB), 1) < iota((NB, NB), 0))
    order_c = jnp.sum(dot(lower, member_c.astype(BF)) * member_c, axis=1, keepdims=True)
    member_r = jnp.where(moving_r & (dest_r == iota((16, NB), 0)), 1.0, 0.0)
    upper = onehot(iota((NB, NB), 0) < iota((NB, NB), 1))
    order_r = jnp.sum(dot(member_r.astype(BF), upper) * member_r, axis=0, keepdims=True)
    key_c = jnp.where(moving_c, dest_c * 16 + order_c.astype(I32), -1000)
    key_r = jnp.where(moving_r, dest_r * 16 + order_r.astype(I32), -1000)

    def table_name(shape, dim):
        r = iota(shape, dim)
        b = r & 31
        return jnp.where(b < MB, b * 8 + lax.shift_right_arithmetic(r, 5), -7)

    send_hot = [onehot(key_r + 8 * h == iota((128, NB), 0)) for h in range(2)]
    back_hot = [onehot(key_c + 8 * h == iota((NB, 128), 1)) for h in range(2)]
    stay_c = onehot((cell_c == table_name((NB, 256), 1)) & jnp.logical_not(moving_c))
    stay_r = onehot((cell_r == table_name((256, NB), 0)) & jnp.logical_not(moving_r))

    red[...] = dot(fine[...], wd[...]).astype(BF)
    for pair in range(4):
        out = sum(dot(send_hot[h], red[(2 * pair + h) * NB:(2 * pair + h + 1) * NB, :]) for h in range(2))
        out = out.astype(BF)
        for d in range(8):
            osnd[d, pair * 16:(pair + 1) * 16, :] = out[d * 16:(d + 1) * 16]
    tags = jnp.broadcast_to((cell_c + 1).astype(F32), (NB, 256)).astype(BF)
    out = (dot(send_hot[0], tags) + dot(send_hot[1], tags)).astype(BF)
    for d in range(8):
        osnd[d, 64:80, :] = out[d * 16:(d + 1) * 16]

    pl.semaphore_wait(barrier, len(peers))
    octs = [remote(osnd.at[d], orcv.at[d], osem, d, at(*DIRS[d])) for d in range(8)]
    for c in octs:
        c.start()

    quad_c = lax.shift_right_arithmetic(iota((128, 128), 0), 5)
    lane = iota((128, 128), 1)

    def names(v):
        owner = ninth(lax.shift_right_arithmetic(v, 1))
        return v - owner * MB, (v >= 0) & (owner == myself), (v >= 0) & (owner != myself)

    for k in range(6):
        vc = nbc[:, k:k + 1]
        vr = nbr[k:k + 1, :]
        idx_c, home_c, far_c = names(vc)
        idx_r, home_r, far_r = names(vr)
        less = far_r & (vr < vc) & (lane < 32)
        rank_c = jnp.sum(jnp.where(less, 1.0, 0.0), axis=1, keepdims=True).astype(I32)
        selp[k, :, 0:128] = onehot(home_c & (idx_c + 32 * quad_c == lane))
        selp[k, :, 128:256] = onehot(far_c & (rank_c + 8 * quad_c == lane))
        early = far_c[0:32] & (iota((32, 128), 0) < (iota((32, 128), 1) & 31))
        rank_r = jnp.sum(jnp.where(early, 1.0, 0.0), axis=0, keepdims=True).astype(I32)
        slot = rank_r + 8 * lax.shift_right_arithmetic(iota((32, 128), 1), 5)
        selc[k] = onehot(far_r & (slot == iota((32, 128), 0)))

    face_to = (at(1, 0), at(-1, 0), at(0, 1), at(0, -1), other)

    def send_faces(ext, snd, rcv, sems):
        for k in range(4):
            for q in range(4):
                snd[k, q * 32:(q + 1) * 32, :] = dot(selc[OPP[k + 1] - 1], layer_quad(ext, k, q)).astype(BF)
        for q in range(4):
            both = dot(selc[5], layer_quad(ext, 4, q)) + dot(selc[4], layer_quad(ext, 5, q))
            snd[4, q * 32:(q + 1) * 32, :] = both.astype(BF)
        copies = [remote(snd.at[k], rcv.at[k], sems, k, face_to[k]) for k in range(5)]
        for c in copies:
            c.start()
        return copies

    def take_faces(ext, rcv, copies):
        for c in copies:
            c.wait_recv()
        for k in range(6):
            for q in range(4):
                near = dot(selp[k, :, 0:128], layer_quad(ext, k, q))
                far = dot(selp[k, :, 128:160], rcv[min(k, 4), q * 32:(q + 1) * 32, :])
                put_halo(ext, k, q, (near + far).astype(BF))

    cot_in.wait()
    cot_faces = send_faces(cotx, fsnd, frcv, fsem)
    fine_t[...] = fine[...].T
    take_faces(cotx, frcv, cot_faces)

    def back_conv(x, carry):
        acc = dot_nt(view(cotx, x, 0), wc[0])
        for d in range(1, 7):
            acc = acc + dot_nt(view(cotx, x, OPP[d]), wc[d])
        gh[x] = acc
        return carry

    lax.fori_loop(0, 4, back_conv, 0)

    for c in octs:
        c.wait_recv()
    tag = orcv[:, 64:80, :].reshape(128, 256).astype(F32)
    row_half = lax.shift_right_arithmetic(iota((128, 256), 0), 3) & 1
    match = tag - 1.0 == table_name((128, 256), 1).astype(F32)
    came = [jnp.where(match & (row_half == h), 1.0, 0.0) for h in range(2)]
    came_t = [m.T.astype(BF) for m in came]
    came = [m.astype(BF) for m in came]
    for c in range(8):
        i, j, k = c >> 2, (c >> 1) & 1, c & 1
        pair = c >> 1
        got = orcv[:, pair * 16:(pair + 1) * 16, :].reshape(128, 256)
        pre = dot(came_t[c & 1], got) + dot(stay_r, red[c * NB:(c + 1) * NB, :])
        sig = 1.0 / (1.0 + jnp.exp(-pre))
        hid = (pre * sig).astype(BF)
        slope = sig * (1.0 + pre * (1.0 - sig))
        for o in range(8):
            x, y, z = 2 * (o >> 2) + i, 2 * ((o >> 1) & 1) + j, 2 * (o & 1) + k
            rows = slice(o * BP, (o + 1) * BP)
            hidx[1 + x, 1 + y, BP * (1 + z):BP * (2 + z), :] = hid[rows]
            grad = gh[x, (y * 4 + z) * BP:(y * 4 + z + 1) * BP, :]
            gbuf[c, rows, :] = (grad * slope[rows]).astype(BF)

    for pair in range(4):
        out = (dot(came[0], gbuf[2 * pair]) + dot(came[1], gbuf[2 * pair + 1])).astype(BF)
        for d in range(8):
            rsnd[d, pair * 16:(pair + 1) * 16, :] = out[d * 16:(d + 1) * 16]
    rets = [remote(rsnd.at[d], rrcv.at[d], rsem, d, at(-DIRS[d][0], -DIRS[d][1])) for d in range(8)]
    for c in rets:
        c.start()
    hid_faces = send_faces(hidx, hsnd, hrcv, hsem)

    for x in range(4):
        hid_t[:, x * 512:(x + 1) * 512] = view(hidx, x, 0).T
    for d in range(7):
        acc = dot(hid_t[:, 0:512], view(cotx, 0, OPP[d]))
        for x in range(1, 4):
            acc = acc + dot(hid_t[:, x * 512:(x + 1) * 512], view(cotx, x, OPP[d]))
        acc = acc.astype(BF)
        for h in range(2):
            pa[h, d * 256:(d + 1) * 256, :] = acc[:, h * 128:(h + 1) * 128]
    core_a = remote(pa.at[1 - gz], ca, coresem, 0, other)
    core_a.start()

    for c in rets:
        c.wait_recv()
    for c in range(8):
        back = rrcv[:, (c >> 1) * 16:(c >> 1) * 16 + 16, :].reshape(128, 256)
        gr[c * NB:(c + 1) * NB, :] = (dot(stay_c, gbuf[c]) + dot(back_hot[c & 1], back)).astype(BF)
    for m in range(4):
        acc = dot(fine_t[m * 256:(m + 1) * 256, :], gr[...]).astype(BF)
        for h in range(2):
            pd[h, m * 256:(m + 1) * 256, :] = acc[:, h * 128:(h + 1) * 128]
    core_d = remote(pd.at[1 - gz], cd, coresem, 1, other)
    core_d.start()

    def x_start(core, p, cbuf, q, xbuf, n, s):
        core.wait_recv()
        q[...] = (p[gz].astype(F32) + cbuf[...].astype(F32)).astype(BF)
        copies = []
        for k in range(1, NX):
            to = at(k, 0)
            copies.append(remote(q.at[pl.ds(pl.multiple_of(to[0] * n, 16), n)], xbuf.at[k], xsem, s * NX + k, to))
        for c in copies:
            c.start()
        return copies

    def z_start(copies, q, xbuf, zbuf, ybuf, n, s):
        for c in copies:
            c.wait_recv()
        acc = q[pl.ds(pl.multiple_of(gx * n, 16), n), :].astype(F32)
        for k in range(1, NX):
            acc = acc + xbuf[k].astype(F32)
        units = n // 16
        zbuf[0:units] = acc.astype(BF).reshape(units, 16, 128)
        zbuf[units:8] = jnp.zeros((8 - units, 16, 128), BF)
        out = []
        for k in range(1, NY):
            to = at(0, k)
            out.append(remote(zbuf.at[to[1]], ybuf.at[k], zsem, s * NY + k, to))
        for c in out:
            c.start()
        return out

    def zg_start(copies, zbuf, ybuf, wbuf, s):
        for c in copies:
            c.wait_recv()
        acc = zbuf[gy].astype(F32)
        for k in range(1, NY):
            acc = acc + ybuf[k].astype(F32)
        wbuf[gy] = acc.astype(BF)
        out = [remote(wbuf.at[gy], wbuf.at[gy], zgsem, s * NY + k, at(0, k)) for k in range(1, NY)]
        for c in out:
            c.start()
        return out

    def xg_start(copies, wbuf, g, n, s):
        for c in copies:
            c.wait_recv()
        mine = pl.ds(pl.multiple_of(gx * n, 16), n)
        g[gz, mine, :] = wbuf[0:n // 16].reshape(n, 128)
        out = [remote(g.at[gz, mine], g.at[gz, mine], xgsem, s * NX + k, at(k, 0)) for k in range(1, NX)]
        for c in out:
            c.start()
        return out

    def cg_start(copies, g, s):
        for c in copies:
            c.wait_recv()
        out = remote(g.at[gz], g.at[gz], cgsem, s, other)
        out.start()
        return out

    xs_a = x_start(core_a, pa, ca, qa, xa, KA, 0)
    xs_d = x_start(core_d, pd, cd, qd, xd, KD, 1)

    take_faces(hidx, hrcv, hid_faces)

    def conv(x, carry):
        acc = dot(view(hidx, x, 0), wc[0])
        for d in range(1, 7):
            acc = acc + dot(view(hidx, x, d), wc[d])
        coarse_o[x] = acc.astype(BF)
        return carry

    lax.fori_loop(0, 4, conv, 0)
    zs_a = z_start(xs_a, qa, xa, za, ya, KA, 0)
    zs_d = z_start(xs_d, qd, xd, zd, yd, KD, 1)
    fineg_o[...] = dot_nt(gr[...], wd[...]).astype(BF)

    zg_a = zg_start(zs_a, za, ya, wa, 0)
    zg_d = zg_start(zs_d, zd, yd, wdn, 1)
    xg_a = xg_start(zg_a, wa, ga, KA, 0)
    xg_d = xg_start(zg_d, wdn, gd, KD, 1)
    cg_a = cg_start(xg_a, ga, 0)
    cg_d = cg_start(xg_d, gd, 1)
    cg_a.wait_recv()
    cg_d.wait_recv()

    for c in (octs + cot_faces + rets + hid_faces + [core_a, core_d] + xs_a + xs_d + zs_a + zs_d
              + zg_a + zg_d + xg_a + xg_d + [cg_a, cg_d]):
        c.wait_send()


def shards(fine_field, target, neighbour, down_weight, conv_weight, out_cotangent):
    fine = fine_field.reshape(NB, 8, 1024).transpose(1, 0, 2).reshape(8 * NB, 1024)
    cot = jnp.pad(out_cotangent.transpose(1, 2, 3, 0, 4), ((0, 0), (0, 0), (0, 0), (0, BP - MB), (0, 0)))
    cot = cot.reshape(4, 4, 4 * BP, 256)
    nb = jnp.pad(neighbour, ((0, BP - MB), (0, 2)), constant_values=-1)
    nbc = jnp.tile(nb, (4, 1))
    vmem = pl.BlockSpec(memory_space=pltpu.VMEM)
    dma = pltpu.SemaphoreType.DMA
    coarse, fineg, ga, gd = pl.pallas_call(
        kernel,
        out_shape=(
            jax.ShapeDtypeStruct((4, 512, 256), BF),
            jax.ShapeDtypeStruct((8 * NB, 1024), BF),
            jax.ShapeDtypeStruct((2, 1792, 128), BF),
            jax.ShapeDtypeStruct((2, 1024, 128), BF),
        ),
        in_specs=[vmem] * 7 + [pl.BlockSpec(memory_space=pl.ANY)],
        out_specs=[vmem] * 4,
        scratch_shapes=[
            pltpu.VMEM((6, 6, 6 * BP, 256), BF),
            pltpu.VMEM((6, 6, 6 * BP, 256), BF),
            pltpu.VMEM((4, 512, 256), F32),
            pltpu.VMEM((8 * NB, 256), BF),
            pltpu.VMEM((1024, 8 * NB), BF),
            pltpu.VMEM((256, 2048), BF),
            pltpu.VMEM((8, 256, 256), BF),
            pltpu.VMEM((8 * NB, 256), BF),
            pltpu.VMEM((6, 32, 128), BF),
            pltpu.VMEM((6, 128, 256), BF),
            pltpu.VMEM((8, 80, 256), BF),
            pltpu.VMEM((8, 80, 256), BF),
            pltpu.VMEM((8, 64, 256), BF),
            pltpu.VMEM((8, 64, 256), BF),
            pltpu.VMEM((5, 128, 256), BF),
            pltpu.VMEM((5, 128, 256), BF),
            pltpu.VMEM((5, 128, 256), BF),
            pltpu.VMEM((5, 128, 256), BF),
            pltpu.VMEM((2, 1792, 128), BF),
            pltpu.VMEM((2, 1024, 128), BF),
            pltpu.VMEM((1792, 128), BF),
            pltpu.VMEM((1024, 128), BF),
            pltpu.VMEM((1792, 128), BF),
            pltpu.VMEM((1024, 128), BF),
            pltpu.VMEM((NX, KA, 128), BF),
            pltpu.VMEM((NX, KD, 128), BF),
            pltpu.VMEM((NY, 16, 128), BF),
            pltpu.VMEM((NY, 16, 128), BF),
            pltpu.VMEM((NY, 16, 128), BF),
            pltpu.VMEM((NY, 16, 128), BF),
            pltpu.VMEM((NY, 16, 128), BF),
            pltpu.VMEM((NY, 16, 128), BF),
            dma,
            dma((2, 8)),
            dma((2, 8)),
            dma((2, 5)),
            dma((2, 5)),
            dma((2, 2)),
            dma((2, 2 * NX)),
            dma((2, 2 * NY)),
            dma((2, 2 * NY)),
            dma((2, 2 * NX)),
            dma((2, 2)),
        ],
        compiler_params=pltpu.CompilerParams(
            collective_id=0, has_side_effects=True, vmem_limit_bytes=56 * 1024 * 1024),
        cost_estimate=pl.CostEstimate(flops=6_000_000_000, bytes_accessed=10_000_000, transcendentals=600_000),
    )(fine, target.reshape(NB, 1), target.reshape(1, NB), nbc, nbc.T, down_weight, conv_weight, cot)

    scale = 1.0 / (64 * MB)
    coarse = coarse.reshape(4, 4, 4, BP, 256)[:, :, :, :MB].transpose(3, 0, 1, 2, 4)
    fineg = fineg.reshape(8, NB, 1024).transpose(1, 0, 2).reshape(NB, 8, 8, 128)
    conv_g = jnp.concatenate([ga[0], ga[1]], axis=1).astype(F32) * scale
    down_g = jnp.concatenate([gd[0], gd[1]], axis=1).astype(F32) * scale
    return coarse, fineg, down_g, conv_g.reshape(7, 256, 256)


def solution(mesh):
    every = ("gx", "gy", "gz")
    in_specs = (
        P(every, None, None, None),
        P(every),
        P(every, None),
        P(),
        P(),
        P(every, None, None, None, None),
    )
    out_specs = (
        P(every, None, None, None, None),
        P(every, None, None, None),
        P(),
        P(),
    )
    return jax.shard_map(shards, mesh=mesh, in_specs=in_specs, out_specs=out_specs, check_vma=False)
```

time: 708 us -> 79.8 us (0.11); the launches traced: 695 us -> 79.5 us
  waiting for transfers between devices: 319 us -> 0 us
  starting transfers between devices: 153 us -> 0 us
  local copies, waits for them, and re-layouts: 153 us -> 12.6 us
  Pallas kernels: 0 us -> 63.7 us
  matrix products: 27.3 us -> 0 us
  other arithmetic: 26.7 us -> 2.46 us
  between operations: 15.6 us -> 0.71 us
    psum x1 -> x0, waiting for transfers between devices: 269 us -> none  [shards(): lax.psum((down_local, conv_local), ('gx', 'gy', 'gz'))]
    ppermute x36 -> x0, starting transfers between devices: 153 us -> none  [from_behind(): return lax.ppermute(array, axis, pairs)]
    pallas_call x0 -> x1, Pallas kernels: none -> 63.7 us  [shards(): pl.pallas_call(kernel, out_shape=(jax.ShapeDtypeStruct((4, 512, 256), BF)...]
    gather x27 -> x0, local copies, waits for them, and re-layouts: 54 us -> none  [the longest x12 27.2 us: collect_faces(): local_face = own_layer[safe_slot]]
    ppermute x36 -> x0, waiting for transfers between devices: 50.5 us -> none  [from_behind(): return lax.ppermute(array, axis, pairs)]
    dot_general x24 -> x0, matrix products: 27.3 us -> none  [the longest x7 10.8 us: shards(): lax.dot_general(flatten_rows(hidden_views[direction]), grad_rows, (((0,),...]
    reshape x16 -> x4, local copies, waits for them, and re-layouts: 23.3 us -> 5.16 us  [the longest x2 2.36 us: shards(): fine_field.reshape(NB, 8, 1024).transpose(1, 0, 2).reshape(8 * NB, 1024)]
    unnamed x135 -> x13, local copies, waits for them, and re-layouts: 19.4 us -> 3.3 us
  transfers between devices with their start and end apart: 37 -> 0, of which waited for: 18 -> 0; matrix products, arithmetic and copies ran while one was open for 24% -> 0% of each run, Pallas kernels for 0% -> 0%
where the time goes in v1:
time: 79.8 us; the launch traced here: 79.5 us
  Pallas kernels  63.7 us (80%)
  local copies, waits for them, and re-layouts  12.6 us (16%)
  other arithmetic  2.46 us (3%)
    pallas_call x1, Pallas kernels, shards(): pl.pallas_call(kernel, out_shape=(jax.ShapeDtypeStruct((4, 512, 256), BF)...  63.7 us
    unnamed x13, local copies, waits for them, and re-layouts  3.3 us
    reshape x2, local copies, waits for them, and re-layouts, shards(): fine_field.reshape(NB, 8, 1024).transpose(1, 0, 2).reshape(8 * NB, 1024)  2.36 us

profile of v1, /device:TPU:1, one launch (start us, length us, event | category | flops | bytes accessed | tf_op | source)
XLA Modules:
  0.0 79.5 jit_solution(2200464084523993858)
XLA Ops:
  0.6 0.0 copy-start
  0.6 0.8 %pad.8 = s32[32,8]{0,1:T(8,128)S(1)} pad(s32[18,6]{0,1:T(8,128)} %param.8, s32[]{:T(128)} %constant.3.clone.1), padding=0_14x0_2 | pad | bytes 1460 | tf_op jit(solution)/shard_map/jit(_pad)/pad | solution.py:360
  1.4 0.1 tile.10
  1.5 1.4 %copy.12.tgtc = s32[80,1]{1,0:T(8,128)} copy(s32[80,1]{0,1:T(1,128)} %bitcast.41) | data formatting | bytes 640 | tf_op jit(solution)/shard_map/reshape | solution.py:422
  2.9 0.7 copy.13.nbc
  3.6 1.4 %copy.18 = bf16[4,4,4,18,256]{4,3,2,1,0:T(8,128)(2,1)S(1)} copy(bf16[4,4,4,18,256]{4,2,1,0,3:T(4,128)(2,1)} %bitcast.38) | data formatting | bytes 1179648
  5.0 1.1 %pad.9.clone = bf16[4,4,4,32,256]{4,3,2,1,0:T(8,128)(2,1)} pad(bf16[4,4,4,18,256]{4,3,2,1,0:T(8,128)(2,1)S(1)} %copy.18, bf16[]{:T(256)} %constant.1.clone.1), padding=0_0x0_0x0_0x0_14x0_0 | pad | bytes 1638402 | tf_op jit(solution)/shard_map/jit(_pad)/pad | solution.py:358
  6.1 0.0 copy-done
  6.1 0.6 reshape.41
  6.7 0.0 copy-done.4
  6.7 1.8 %copy.10 = bf16[80,8,1024]{2,0,1:T(8,128)(2,1)} copy(bf16[80,8,1024]{2,1,0:T(8,128)(2,1)S(1)} %reshape.41) | data formatting | bytes 2621440 | tf_op jit(solution)/shard_map/reshape | solution.py:357
  8.5 63.7 %shard_map.93 = (bf16[4,512,256]{2,1,0:T(8,128)(2,1)}, bf16[640,1024]{1,0:T(8,128)(2,1)}, bf16[2,1792,128]{2,1,0:T(8,128)(2,1)}, bf16[2,1024,128]{2,1,0:T(8,128)(2,1)}) custom-call(bf16[640,1024]{1,0:T(8,128)(2,1)} %bitcast.35, s32[80,1]{1,0:T(8,128)} %copy.12.tgtc, s32[1,80]{1,0:T(1,128)} %bitcast.42, s32[128,8]{1,0:T(8,128)} %copy.13.nbc, ...), custom_call_target="tpu_custom_call" | custom-call | flops 6000000000 | bytes 10000000 | tf_op jit(solution)/shard_map/pallas_call | solution.py:364
  72.3 0.0 copy-start.1
  72.3 1.3 %slice.20 = bf16[4,4,4,18,256]{4,3,2,1,0:T(8,128)(2,1)S(1)} slice(bf16[4,4,4,32,256]{4,3,2,1,0:T(8,128)(2,1)} %bitcast.37), slice={[0:4], [0:4], [0:4], [0:18], [0:256]} | slice | bytes 1179648 | tf_op jit(solution)/shard_map/slice | solution.py:425
  73.6 1.1 %copy.21 = bf16[4,4,4,18,256]{4,2,1,0,3:T(4,128)(2,1)} copy(bf16[4,4,4,18,256]{4,3,2,1,0:T(8,128)(2,1)S(1)} %slice.20) | data formatting | bytes 1179648
  74.7 0.0 copy-done.1
  74.7 0.4 copy.19
  75.1 0.0 copy-start.3
  75.1 1.4 %copy.16 = bf16[80,8,8,128]{3,2,1,0:T(8,128)(2,1)} copy(bf16[80,8,8,128]{3,2,0,1:T(8,128)(2,1)S(1)} %bitcast.31) | data formatting | bytes 2621440 | tf_op jit(solution)/shard_map/reshape | solution.py:426
  76.5 0.0 copy-done.3
  76.6 1.1 %convert_multiply_fusion.1 = f32[1024,256]{1,0:T(8,128)} fusion(bf16[1024,128]{1,0:T(8,128)(2,1)S(1)} %get-tuple-element.15, bf16[1024,128]{1,0:T(8,128)(2,1)S(1)} %get-tuple-element.14), kind=kLoop, calls=%fused_computation.1 | loop fusion | flops 1310720 | bytes 1572864 | tf_op jit(solution)/shard_map/mul | solution.py:428
  77.6 0.4 copy-done.2
  78.0 0.1 fusion
  78.1 1.4 %convert_multiply_fusion = f32[7,256,256]{2,1,0:T(8,128)} fusion(bf16[7,256,128]{2,1,0:T(8,128)(2,1)S(1)} %bitcast.33, bf16[7,256,128]{2,1,0:T(8,128)(2,1)S(1)} %bitcast.32), kind=kLoop, calls=%fused_computation | loop fusion | flops 2293760 | bytes 2752512 | tf_op jit(solution)/shard_map/mul | solution.py:427
  (4 shorter events, 0.0 us)
Async XLA Ops:
  0.6 5.5 %copy-start = (bf16[80,8,8,128]{3,2,1,0:T(8,128)(2,1)S(1)}, bf16[80,8,8,128]{3,2,1,0:T(8,128)(2,1)}, u32[]{:S(2)}) copy-start(bf16[80,8,8,128]{3,2,1,0:T(8,128)(2,1)} %param.6) | copy-start | bytes 3932164
  1.5 5.2 %copy-start.4 = (s32[128,8]{0,1:T(8,128)}, s32[128,8]{0,1:T(8,128)S(1)}, u32[]{:S(2)}) copy-start(s32[128,8]{0,1:T(8,128)S(1)} %tile.10) | copy-start | bytes 12292
  72.3 2.4 %copy-start.1 = (bf16[640,1024]{1,0:T(8,128)(2,1)S(1)}, bf16[640,1024]{1,0:T(8,128)(2,1)}, u32[]{:S(2)}) copy-start(bf16[640,1024]{1,0:T(8,128)(2,1)} %get-tuple-element.9) | copy-start | bytes 3932164
  75.1 1.4 %copy-start.3 = (bf16[2,1024,128]{2,1,0:T(8,128)(2,1)S(1)}, bf16[2,1024,128]{2,1,0:T(8,128)(2,1)}, u32[]{:S(2)}) copy-start(bf16[2,1024,128]{2,1,0:T(8,128)(2,1)} %get-tuple-element.10) | copy-start | bytes 1572868
  76.5 1.5 %copy-start.2 = (bf16[2,1792,128]{2,1,0:T(8,128)(2,1)S(1)}, bf16[2,1792,128]{2,1,0:T(8,128)(2,1)}, u32[]{:S(2)}) copy-start(bf16[2,1792,128]{2,1,0:T(8,128)(2,1)} %get-tuple-element.11) | copy-start | bytes 2752516

commit v2 on v1

--- a/solution.py
+++ b/solution.py
@@ -77,12 +77,13 @@
         ext[1 + q, 1:5, BP * z:BP * (z + 1), :] = rows.reshape(4, BP, 256)
 
 
-def kernel(fine, tgtc, tgtr, nbc, nbr, wd, wc, cot,
-           coarse_o, fineg_o, ga, gd,
-           cotx, hidx, gh, red, fine_t, hid_t, gbuf, gr, selc, selp,
+def kernel(fine_h, tgt, nb, wd_h, wc_h, cot_h,
+           coarse_h, fineg_h, ga, gd,
+           fin, cin, wd, wc, wt, t_scr, n_scr, wide, tall, fine, coarse_v, fineg_v,
+           cotx, hidx, gh, red, slope, fine_t, hid_t, gr, selc, selp,
            osnd, orcv, rsnd, rrcv, fsnd, frcv, hsnd, hrcv,
-           pa, pd, ca, cd, qa, qd, xa, xd, za, zd, ya, yd, wa, wdn,
-           csem, osem, rsem, fsem, hsem, coresem, xsem, zsem, zgsem, xgsem, cgsem):
+           pa, pd, ca, cd, qa, qd, xa, xd, za, ya, yd, wa,
+           isem, esem, osem, rsem, fsem, hsem, coresem, xsem, zsem, zgsem, xgsem, cgsem):
     gx, gy, gz = lax.axis_index("gx"), lax.axis_index("gy"), lax.axis_index("gz")
     myself = (gx * NY + gy) * NZ + gz
 
@@ -97,13 +98,79 @@
     for peer in peers:
         pl.semaphore_signal(barrier, inc=1, device_id=peer, device_id_type=MESH)
 
-    cot_in = pltpu.make_async_copy(cot, cotx.at[1:5, 1:5, BP:5 * BP, :], csem)
-    cot_in.start()
+    loads = [pltpu.make_async_copy(src, dst, isem.at[i]) for i, (src, dst) in enumerate(
+        ((cot_h, cin), (fine_h, fin), (wd_h, wd), (wc_h, wc)))]
+    for c in loads:
+        c.start()
 
     def remote(src, dst, sems, i, device):
         return pltpu.make_async_remote_copy(
             src_ref=src, dst_ref=dst, send_sem=sems.at[0, i], recv_sem=sems.at[1, i],
             device_id=device, device_id_type=MESH)
+
+    quad_c = lax.shift_right_arithmetic(iota((128, 128), 0), 5)
+    lane = iota((128, 128), 1)
+
+    n_scr[...] = jnp.full((8, 128), -1, I32)
+    for q in range(4):
+        n_scr[0:6, BP * q:BP * q + MB] = nb[...]
+    nb_r = n_scr[...]
+    nb_c = nb_r.T
+
+    def names(v):
+        owner = ninth(lax.shift_right_arithmetic(v, 1))
+        return v - owner * MB, (v >= 0) & (owner == myself), (v >= 0) & (owner != myself)
+
+    for k in range(6):
+        vc = nb_c[:, k:k + 1]
+        vr = nb_r[k:k + 1, :]
+        idx_c, home_c, far_c = names(vc)
+        idx_r, home_r, far_r = names(vr)
+        less = far_r & (vr < vc) & (lane < 32)
+        rank_c = jnp.sum(jnp.where(less, 1.0, 0.0), axis=1, keepdims=True).astype(I32)
+        selp[k, :, 0:128] = onehot(home_c & (idx_c + 32 * quad_c == lane))
+        selp[k, :, 128:256] = onehot(far_c & (rank_c + 8 * quad_c == lane))
+        early = far_c[0:32] & (iota((32, 128), 0) < (iota((32, 128), 1) & 31))
+        rank_r = jnp.sum(jnp.where(early, 1.0, 0.0), axis=0, keepdims=True).astype(I32)
+        slot = rank_r + 8 * lax.shift_right_arithmetic(iota((32, 128), 1), 5)
+        selc[k] = onehot(far_r & (slot == iota((32, 128), 0)))
+
+    face_to = (at(1, 0), at(-1, 0), at(0, 1), at(0, -1), other)
+
+    def send_faces(ext, snd, rcv, sems):
+        for k in range(4):
+            for q in range(4):
+                snd[k, q * 32:(q + 1) * 32, :] = dot(selc[OPP[k + 1] - 1], layer_quad(ext, k, q)).astype(BF)
+        for q in range(4):
+            both = dot(selc[5], layer_quad(ext, 4, q)) + dot(selc[4], layer_quad(ext, 5, q))
+            snd[4, q * 32:(q + 1) * 32, :] = both.astype(BF)
+        copies = [remote(snd.at[k], rcv.at[k], sems, k, face_to[k]) for k in range(5)]
+        for c in copies:
+            c.start()
+        return copies
+
+    def take_faces(ext, rcv, copies):
+        for c in copies:
+            c.wait_recv()
+        for k in range(6):
+            for q in range(4):
+                near = dot(selp[k, :, 0:128], layer_quad(ext, k, q))
+                far = dot(selp[k, :, 128:160], rcv[min(k, 4), q * 32:(q + 1) * 32, :])
+                put_halo(ext, k, q, (near + far).astype(BF))
+
+    loads[0].wait()
+    tall[...] = jnp.zeros_like(tall)
+    for m in range(16 * MB):
+        part = cin[m].astype(F32)
+        for h in range(2):
+            tall[h, 4 * m:4 * m + 4, :] = part[:, h * 128:(h + 1) * 128]
+    for p in range(64):
+        x, y, z = p >> 4, (p >> 2) & 3, p & 3
+        for h in range(2):
+            rows = tall[h, pl.ds(p, BP, stride=64), :]
+            cotx[1 + x, 1 + y, BP * (1 + z):BP * (2 + z), h * 128:(h + 1) * 128] = rows.astype(BF)
+    pl.semaphore_wait(barrier, len(peers))
+    cot_faces = send_faces(cotx, fsnd, frcv, fsem)
 
     def place(t):
         owner = ninth(lax.shift_right_arithmetic(t, 4))
@@ -114,8 +181,9 @@
         flat = (sx + 1) * 3 + (sy + 1)
         return cell, moving, jnp.where(flat > 4, flat - 1, flat)
 
-    cell_c, moving_c, dest_c = place(tgtc[...])
-    cell_r, moving_r, dest_r = place(tgtr[...])
+    t_scr[:, 0:NB] = jnp.broadcast_to(tgt[...], (128, NB))
+    cell_c, moving_c, dest_c = place(t_scr[...].T[0:NB, 0:1])
+    cell_r, moving_r, dest_r = place(tgt[...])
     member_c = jnp.where(moving_c & (dest_c == iota((NB, 128), 1)), 1.0, 0.0)
     lower = onehot(iota((NB, NB), 1) < iota((NB, NB), 0))
     order_c = jnp.sum(dot(lower, member_c.astype(BF)) * member_c, axis=1, keepdims=True)
@@ -135,6 +203,13 @@
     stay_c = onehot((cell_c == table_name((NB, 256), 1)) & jnp.logical_not(moving_c))
     stay_r = onehot((cell_r == table_name((256, NB), 0)) & jnp.logical_not(moving_r))
 
+    loads[1].wait()
+    wide[...] = fin[...].astype(F32)
+    for c in range(8):
+        for v in range(8):
+            part = wide[pl.ds(c * 8 + v, NB, stride=64), :]
+            fine[c * NB:(c + 1) * NB, v * 128:(v + 1) * 128] = part.astype(BF)
+    loads[2].wait()
     red[...] = dot(fine[...], wd[...]).astype(BF)
     for pair in range(4):
         out = sum(dot(send_hot[h], red[(2 * pair + h) * NB:(2 * pair + h + 1) * NB, :]) for h in range(2))
@@ -146,65 +221,22 @@
     for d in range(8):
         osnd[d, 64:80, :] = out[d * 16:(d + 1) * 16]
 
-    pl.semaphore_wait(barrier, len(peers))
     octs = [remote(osnd.at[d], orcv.at[d], osem, d, at(*DIRS[d])) for d in range(8)]
     for c in octs:
         c.start()
 
-    quad_c = lax.shift_right_arithmetic(iota((128, 128), 0), 5)
-    lane = iota((128, 128), 1)
-
-    def names(v):
-        owner = ninth(lax.shift_right_arithmetic(v, 1))
-        return v - owner * MB, (v >= 0) & (owner == myself), (v >= 0) & (owner != myself)
-
-    for k in range(6):
-        vc = nbc[:, k:k + 1]
-        vr = nbr[k:k + 1, :]
-        idx_c, home_c, far_c = names(vc)
-        idx_r, home_r, far_r = names(vr)
-        less = far_r & (vr < vc) & (lane < 32)
-        rank_c = jnp.sum(jnp.where(less, 1.0, 0.0), axis=1, keepdims=True).astype(I32)
-        selp[k, :, 0:128] = onehot(home_c & (idx_c + 32 * quad_c == lane))
-        selp[k, :, 128:256] = onehot(far_c & (rank_c + 8 * quad_c == lane))
-        early = far_c[0:32] & (iota((32, 128), 0) < (iota((32, 128), 1) & 31))
-        rank_r = jnp.sum(jnp.where(early, 1.0, 0.0), axis=0, keepdims=True).astype(I32)
-        slot = rank_r + 8 * lax.shift_right_arithmetic(iota((32, 128), 1), 5)
-        selc[k] = onehot(far_r & (slot == iota((32, 128), 0)))
-
-    face_to = (at(1, 0), at(-1, 0), at(0, 1), at(0, -1), other)
-
-    def send_faces(ext, snd, rcv, sems):
-        for k in range(4):
-            for q in range(4):
-                snd[k, q * 32:(q + 1) * 32, :] = dot(selc[OPP[k + 1] - 1], layer_quad(ext, k, q)).astype(BF)
-        for q in range(4):
-            both = dot(selc[5], layer_quad(ext, 4, q)) + dot(selc[4], layer_quad(ext, 5, q))
-            snd[4, q * 32:(q + 1) * 32, :] = both.astype(BF)
-        copies = [remote(snd.at[k], rcv.at[k], sems, k, face_to[k]) for k in range(5)]
-        for c in copies:
-            c.start()
-        return copies
-
-    def take_faces(ext, rcv, copies):
-        for c in copies:
-            c.wait_recv()
-        for k in range(6):
-            for q in range(4):
-                near = dot(selp[k, :, 0:128], layer_quad(ext, k, q))
-                far = dot(selp[k, :, 128:160], rcv[min(k, 4), q * 32:(q + 1) * 32, :])
-                put_halo(ext, k, q, (near + far).astype(BF))
-
-    cot_in.wait()
-    cot_faces = send_faces(cotx, fsnd, frcv, fsem)
     fine_t[...] = fine[...].T
+    pre = red[...].astype(F32)
+    sig = 1.0 / (1.0 + jnp.exp(-pre))
+    slope[...] = sig * (1.0 + pre * (1.0 - sig))
+    loads[3].wait()
+    for d in range(7):
+        wt[d * 256:(d + 1) * 256, :] = wc[d * 256:(d + 1) * 256, :].T
     take_faces(cotx, frcv, cot_faces)
 
     def back_conv(x, carry):
-        acc = dot_nt(view(cotx, x, 0), wc[0])
-        for d in range(1, 7):
-            acc = acc + dot_nt(view(cotx, x, OPP[d]), wc[d])
-        gh[x] = acc
+        rows = jnp.concatenate([view(cotx, x, OPP[d]) for d in range(7)], axis=1)
+        gh[x] = dot(rows, wt[...]).astype(BF)
         return carry
 
     lax.fori_loop(0, 4, back_conv, 0)
@@ -217,37 +249,39 @@
     came = [jnp.where(match & (row_half == h), 1.0, 0.0) for h in range(2)]
     came_t = [m.T.astype(BF) for m in came]
     came = [m.astype(BF) for m in came]
+
+    def grads(c):
+        i, j, k = c >> 2, (c >> 1) & 1, c & 1
+        out = []
+        for o in range(8):
+            x, y, z = 2 * (o >> 2) + i, 2 * ((o >> 1) & 1) + j, 2 * (o & 1) + k
+            out.append(gh[x, (y * 4 + z) * BP:(y * 4 + z + 1) * BP, :])
+        return jnp.concatenate(out, axis=0)
+
+    for pair in range(4):
+        out = (dot(came[0], grads(2 * pair)) + dot(came[1], grads(2 * pair + 1))).astype(BF)
+        for d in range(8):
+            rsnd[d, pair * 16:(pair + 1) * 16, :] = out[d * 16:(d + 1) * 16]
+    rets = [remote(rsnd.at[d], rrcv.at[d], rsem, d, at(-DIRS[d][0], -DIRS[d][1])) for d in range(8)]
+    for c in rets:
+        c.start()
+
     for c in range(8):
         i, j, k = c >> 2, (c >> 1) & 1, c & 1
         pair = c >> 1
         got = orcv[:, pair * 16:(pair + 1) * 16, :].reshape(128, 256)
         pre = dot(came_t[c & 1], got) + dot(stay_r, red[c * NB:(c + 1) * NB, :])
-        sig = 1.0 / (1.0 + jnp.exp(-pre))
-        hid = (pre * sig).astype(BF)
-        slope = sig * (1.0 + pre * (1.0 - sig))
+        hid = (pre / (1.0 + jnp.exp(-pre))).astype(BF)
         for o in range(8):
             x, y, z = 2 * (o >> 2) + i, 2 * ((o >> 1) & 1) + j, 2 * (o & 1) + k
-            rows = slice(o * BP, (o + 1) * BP)
-            hidx[1 + x, 1 + y, BP * (1 + z):BP * (2 + z), :] = hid[rows]
-            grad = gh[x, (y * 4 + z) * BP:(y * 4 + z + 1) * BP, :]
-            gbuf[c, rows, :] = (grad * slope[rows]).astype(BF)
-
-    for pair in range(4):
-        out = (dot(came[0], gbuf[2 * pair]) + dot(came[1], gbuf[2 * pair + 1])).astype(BF)
-        for d in range(8):
-            rsnd[d, pair * 16:(pair + 1) * 16, :] = out[d * 16:(d + 1) * 16]
-    rets = [remote(rsnd.at[d], rrcv.at[d], rsem, d, at(-DIRS[d][0], -DIRS[d][1])) for d in range(8)]
-    for c in rets:
-        c.start()
+            hidx[1 + x, 1 + y, BP * (1 + z):BP * (2 + z), :] = hid[o * BP:(o + 1) * BP]
     hid_faces = send_faces(hidx, hsnd, hrcv, hsem)
 
     for x in range(4):
         hid_t[:, x * 512:(x + 1) * 512] = view(hidx, x, 0).T
     for d in range(7):
-        acc = dot(hid_t[:, 0:512], view(cotx, 0, OPP[d]))
-        for x in range(1, 4):
-            acc = acc + dot(hid_t[:, x * 512:(x + 1) * 512], view(cotx, x, OPP[d]))
-        acc = acc.astype(BF)
+        rows = jnp.concatenate([view(cotx, x, OPP[d]) for x in range(4)], axis=0)
+        acc = dot(hid_t[...], rows).astype(BF)
         for h in range(2):
             pa[h, d * 256:(d + 1) * 256, :] = acc[:, h * 128:(h + 1) * 128]
     core_a = remote(pa.at[1 - gz], ca, coresem, 0, other)
@@ -257,7 +291,8 @@
         c.wait_recv()
     for c in range(8):
         back = rrcv[:, (c >> 1) * 16:(c >> 1) * 16 + 16, :].reshape(128, 256)
-        gr[c * NB:(c + 1) * NB, :] = (dot(stay_c, gbuf[c]) + dot(back_hot[c & 1], back)).astype(BF)
+        grad = dot(stay_c, grads(c)) + dot(back_hot[c & 1], back)
+        gr[c * NB:(c + 1) * NB, :] = (grad * slope[c * NB:(c + 1) * NB, :]).astype(BF)
     for m in range(4):
         acc = dot(fine_t[m * 256:(m + 1) * 256, :], gr[...]).astype(BF)
         for h in range(2):
@@ -322,63 +357,124 @@
         out.start()
         return out
 
+    def zb_start(copies, q, xbuf, ybuf, n, s):
+        for c in copies:
+            c.wait_recv()
+        acc = q[pl.ds(pl.multiple_of(gx * n, 16), n), :].astype(F32)
+        for k in range(1, NX):
+            acc = acc + xbuf[k].astype(F32)
+        ybuf[gy] = acc.astype(BF)
+        out = [remote(ybuf.at[gy], ybuf.at[gy], zsem, s * NY + k, at(0, k)) for k in range(1, NY)]
+        for c in out:
+            c.start()
+        return out
+
+    def xb_start(copies, ybuf, g, n, s):
+        for c in copies:
+            c.wait_recv()
+        acc = ybuf[0].astype(F32)
+        for k in range(1, NY):
+            acc = acc + ybuf[k].astype(F32)
+        mine = pl.ds(pl.multiple_of(gx * n, 16), n)
+        g[gz, mine, :] = acc.astype(BF)
+        out = [remote(g.at[gz, mine], g.at[gz, mine], xgsem, s * NX + k, at(k, 0)) for k in range(1, NX)]
+        for c in out:
+            c.start()
+        return out
+
     xs_a = x_start(core_a, pa, ca, qa, xa, KA, 0)
     xs_d = x_start(core_d, pd, cd, qd, xd, KD, 1)
 
     take_faces(hidx, hrcv, hid_faces)
 
     def conv(x, carry):
-        acc = dot(view(hidx, x, 0), wc[0])
-        for d in range(1, 7):
-            acc = acc + dot(view(hidx, x, d), wc[d])
-        coarse_o[x] = acc.astype(BF)
+        rows = jnp.concatenate([view(hidx, x, d) for d in range(7)], axis=1)
+        acc = dot(rows, wc[...])
+        for p in range(16):
+            for h in range(2):
+                tall[h, pl.ds(x * 16 + p, BP, stride=64), :] = acc[p * BP:(p + 1) * BP, h * 128:(h + 1) * 128]
         return carry
 
     lax.fori_loop(0, 4, conv, 0)
+    for m in range(16 * MB):
+        for h in range(2):
+            coarse_v[m, :, h * 128:(h + 1) * 128] = tall[h, 4 * m:4 * m + 4, :].astype(BF)
+    stores = [pltpu.make_async_copy(coarse_v, coarse_h, esem.at[0])]
+    stores[0].start()
+
     zs_a = z_start(xs_a, qa, xa, za, ya, KA, 0)
-    zs_d = z_start(xs_d, qd, xd, zd, yd, KD, 1)
-    fineg_o[...] = dot_nt(gr[...], wd[...]).astype(BF)
-
+    zs_d = zb_start(xs_d, qd, xd, yd, KD, 1)
     zg_a = zg_start(zs_a, za, ya, wa, 0)
-    zg_d = zg_start(zs_d, zd, yd, wdn, 1)
+    xg_d = xb_start(zs_d, yd, gd, KD, 1)
+
+    for c in range(8):
+        flow = dot_nt(gr[c * NB:(c + 1) * NB, :], wd[...])
+        for v in range(8):
+            wide[pl.ds(c * 8 + v, NB, stride=64), :] = flow[:, v * 128:(v + 1) * 128]
+    fineg_v[...] = wide[...].astype(BF)
+    stores.append(pltpu.make_async_copy(fineg_v, fineg_h, esem.at[1]))
+    stores[1].start()
+
     xg_a = xg_start(zg_a, wa, ga, KA, 0)
-    xg_d = xg_start(zg_d, wdn, gd, KD, 1)
+    cg_d = cg_start(xg_d, gd, 1)
     cg_a = cg_start(xg_a, ga, 0)
-    cg_d = cg_start(xg_d, gd, 1)
+    cg_d.wait_recv()
     cg_a.wait_recv()
-    cg_d.wait_recv()
+    for c in stores:
+        c.wait()
 
     for c in (octs + cot_faces + rets + hid_faces + [core_a, core_d] + xs_a + xs_d + zs_a + zs_d
-              + zg_a + zg_d + xg_a + xg_d + [cg_a, cg_d]):
+              + zg_a + xg_a + xg_d + [cg_a, cg_d]):
         c.wait_send()
 
 
+def finish(coarse_h, fineg_h, ga, gd, coarse_o, fineg_o, down_o, conv_o, sem):
+    copies = [pltpu.make_async_copy(coarse_h, coarse_o, sem.at[0]),
+              pltpu.make_async_copy(fineg_h, fineg_o, sem.at[1])]
+    for c in copies:
+        c.start()
+    scale = 1.0 / (64 * MB)
+    for h in range(2):
+        down_o[:, h * 128:(h + 1) * 128] = gd[h].astype(F32) * scale
+        conv_o[:, h * 128:(h + 1) * 128] = ga[h].astype(F32) * scale
+    for c in copies:
+        c.wait()
+
+
 def shards(fine_field, target, neighbour, down_weight, conv_weight, out_cotangent):
-    fine = fine_field.reshape(NB, 8, 1024).transpose(1, 0, 2).reshape(8 * NB, 1024)
-    cot = jnp.pad(out_cotangent.transpose(1, 2, 3, 0, 4), ((0, 0), (0, 0), (0, 0), (0, BP - MB), (0, 0)))
-    cot = cot.reshape(4, 4, 4 * BP, 256)
-    nb = jnp.pad(neighbour, ((0, BP - MB), (0, 2)), constant_values=-1)
-    nbc = jnp.tile(nb, (4, 1))
     vmem = pl.BlockSpec(memory_space=pltpu.VMEM)
+    anyw = pl.BlockSpec(memory_space=pl.ANY)
     dma = pltpu.SemaphoreType.DMA
     coarse, fineg, ga, gd = pl.pallas_call(
         kernel,
         out_shape=(
-            jax.ShapeDtypeStruct((4, 512, 256), BF),
-            jax.ShapeDtypeStruct((8 * NB, 1024), BF),
+            jax.ShapeDtypeStruct((16 * MB, 4, 256), BF),
+            jax.ShapeDtypeStruct((64 * NB, 128), BF),
             jax.ShapeDtypeStruct((2, 1792, 128), BF),
             jax.ShapeDtypeStruct((2, 1024, 128), BF),
         ),
-        in_specs=[vmem] * 7 + [pl.BlockSpec(memory_space=pl.ANY)],
-        out_specs=[vmem] * 4,
+        in_specs=[anyw, vmem, vmem, anyw, anyw, anyw],
+        out_specs=[anyw, anyw, vmem, vmem],
         scratch_shapes=[
+            pltpu.VMEM((64 * NB, 128), BF),
+            pltpu.VMEM((16 * MB, 4, 256), BF),
+            pltpu.VMEM((1024, 256), BF),
+            pltpu.VMEM((1792, 256), BF),
+            pltpu.VMEM((1792, 256), BF),
+            pltpu.VMEM((128, 128), I32),
+            pltpu.VMEM((8, 128), I32),
+            pltpu.VMEM((64 * NB, 128), F32),
+            pltpu.VMEM((2, 64 * BP, 128), F32),
+            pltpu.VMEM((8 * NB, 1024), BF),
+            pltpu.VMEM((16 * MB, 4, 256), BF),
+            pltpu.VMEM((64 * NB, 128), BF),
             pltpu.VMEM((6, 6, 6 * BP, 256), BF),
             pltpu.VMEM((6, 6, 6 * BP, 256), BF),
-            pltpu.VMEM((4, 512, 256), F32),
+            pltpu.VMEM((4, 512, 256), BF),
             pltpu.VMEM((8 * NB, 256), BF),
+            pltpu.VMEM((8 * NB, 256), F32),
             pltpu.VMEM((1024, 8 * NB), BF),
             pltpu.VMEM((256, 2048), BF),
-            pltpu.VMEM((8, 256, 256), BF),
             pltpu.VMEM((8 * NB, 256), BF),
             pltpu.VMEM((6, 32, 128), BF),
             pltpu.VMEM((6, 128, 256), BF),
@@ -400,11 +496,10 @@
             pltpu.VMEM((NX, KD, 128), BF),
             pltpu.VMEM((NY, 16, 128), BF),
             pltpu.VMEM((NY, 16, 128), BF),
+            pltpu.VMEM((NY, KD, 128), BF),
             pltpu.VMEM((NY, 16, 128), BF),
-            pltpu.VMEM((NY, 16, 128), BF),
-            pltpu.VMEM((NY, 16, 128), BF),
-            pltpu.VMEM((NY, 16, 128), BF),
-            dma,
+            dma((4,)),
+            dma((2,)),
             dma((2, 8)),
             dma((2, 8)),
             dma((2, 5)),
@@ -419,14 +514,24 @@
         compiler_params=pltpu.CompilerParams(
             collective_id=0, has_side_effects=True, vmem_limit_bytes=56 * 1024 * 1024),
         cost_estimate=pl.CostEstimate(flops=6_000_000_000, bytes_accessed=10_000_000, transcendentals=600_000),
-    )(fine, target.reshape(NB, 1), target.reshape(1, NB), nbc, nbc.T, down_weight, conv_weight, cot)
-
-    scale = 1.0 / (64 * MB)
-    coarse = coarse.reshape(4, 4, 4, BP, 256)[:, :, :, :MB].transpose(3, 0, 1, 2, 4)
-    fineg = fineg.reshape(8, NB, 1024).transpose(1, 0, 2).reshape(NB, 8, 8, 128)
-    conv_g = jnp.concatenate([ga[0], ga[1]], axis=1).astype(F32) * scale
-    down_g = jnp.concatenate([gd[0], gd[1]], axis=1).astype(F32) * scale
-    return coarse, fineg, down_g, conv_g.reshape(7, 256, 256)
+    )(fine_field.reshape(64 * NB, 128), target.reshape(1, NB), neighbour.T, down_weight,
+      conv_weight.reshape(1792, 256), out_cotangent.reshape(16 * MB, 4, 256))
+
+    coarse, fineg, down_g, conv_g = pl.pallas_call(
+        finish,
+        out_shape=(
+            jax.ShapeDtypeStruct((16 * MB, 4, 256), BF),
+            jax.ShapeDtypeStruct((64 * NB, 128), BF),
+            jax.ShapeDtypeStruct((1024, 256), F32),
+            jax.ShapeDtypeStruct((1792, 256), F32),
+        ),
+        in_specs=[anyw, anyw, vmem, vmem],
+        out_specs=[anyw, anyw, vmem, vmem],
+        scratch_shapes=[dma((2,))],
+        compiler_params=pltpu.CompilerParams(vmem_limit_bytes=32 * 1024 * 1024),
+    )(coarse, fineg, ga, gd)
+    return (coarse.reshape(MB, 4, 4, 4, 256), fineg.reshape(NB, 8, 8, 128), down_g,
+            conv_g.reshape(7, 256, 256))
 
 
 def solution(mesh):

time: 79.8 us -> 68.2 us (0.85)
  local copies, waits for them, and re-layouts: 12.6 us -> 4.59 us
  other arithmetic: 2.46 us -> 0 us
  Pallas kernels: 63.7 us -> 62.5 us
    reshape x4 -> x0, local copies, waits for them, and re-layouts: 5.16 us -> none  [the longest x2 2.36 us: shards(): fine_field.reshape(NB, 8, 1024).transpose(1, 0, 2).reshape(8 * NB, 1024)]
    mul x2 -> x0, other arithmetic: 2.46 us -> none  [the longest x1 1.41 us: shards(): conv_g = jnp.concatenate([ga[0], ga[1]], axis=1).astype(F32) * scale]
    pad x2 -> x0, local copies, waits for them, and re-layouts: 1.91 us -> none  [the longest x1 1.11 us: shards(): jnp.pad(out_cotangent.transpose(1, 2, 3, 0, 4), ((0, 0), (0, 0), (0, 0),...]
    slice x2 -> x0, local copies, waits for them, and re-layouts: 1.36 us -> none  [the longest x1 1.3 us: shards(): coarse.reshape(4, 4, 4, BP, 256)[:, :, :, :MB].transpose(3, 0, 1, 2, 4)]
    unnamed x13 -> x8, local copies, waits for them, and re-layouts: 3.3 us -> 4.59 us
    pallas_call x1 -> x2, Pallas kernels: 63.7 us -> 62.5 us  [the longest x1 59.6 us: shards(): pl.pallas_call(kernel, out_shape=(jax.ShapeDtypeStruct((16 * MB, 4, 256),...]
    another operation x3 -> x0, local copies, waits for them, and re-layouts: 0.82 us -> none  [shards(): nbc = jnp.tile(nb, (4, 1))]
where the time goes in v2:
time: 68.2 us; the launch traced here: 67.9 us
  Pallas kernels  62.5 us (92%)
  local copies, waits for them, and re-layouts  4.59 us (7%)
  between operations  0.81 us (1%)
    pallas_call x1, Pallas kernels, shards(): pl.pallas_call(kernel, out_shape=(jax.ShapeDtypeStruct((16 * MB, 4, 256),...  59.6 us
    unnamed x8, local copies, waits for them, and re-layouts  4.59 us
    pallas_call x1, Pallas kernels, shards(): pl.pallas_call(finish, out_shape=(jax.ShapeDtypeStruct((16 * MB, 4, 256),...  2.84 us

profile of v2, /device:TPU:1, one launch (start us, length us, event | category | flops | bytes accessed | tf_op | source)
XLA Modules:
  0.0 67.9 jit_solution(7911521402395687444)
XLA Ops:
  0.6 59.6 %shard_map.93 = (bf16[288,4,256]{2,1,0:T(4,128)(2,1)}, bf16[5120,128]{1,0:T(8,128)(2,1)}, bf16[2,1792,128]{2,1,0:T(8,128)(2,1)}, bf16[2,1024,128]{2,1,0:T(8,128)(2,1)}) custom-call(bf16[5120,128]{1,0:T(8,128)(2,1)} %bitcast.9, s32[1,80]{1,0:T(1,128)} %bitcast.15, s32[6,18]{1,0:T(8,128)} %bitcast.14, bf16[1024,256]{1,0:T(8,128)(2,1)} %wd_h.1, ...), custom_call_target="tpu_custom_call" | custom-call | flops 6000000000 | bytes 10000000 | tf_op jit(solution)/shard_map/pallas_call | solution.py:448
  60.3 0.0 copy-start
  60.3 1.3 %copy-done = bf16[5120,128]{1,0:T(8,128)(2,1)S(1)} copy-done((bf16[5120,128]{1,0:T(8,128)(2,1)S(1)}, bf16[5120,128]{1,0:T(8,128)(2,1)}, u32[]{:S(2)}) %copy-start) | copy-done | bytes 1310744
  61.6 0.0 copy-start.1
  61.6 1.2 %copy-done.1 = bf16[2,1792,128]{2,1,0:T(8,128)(2,1)S(1)} copy-done((bf16[2,1792,128]{2,1,0:T(8,128)(2,1)S(1)}, bf16[2,1792,128]{2,1,0:T(8,128)(2,1)}, u32[]{:S(2)}) %copy-start.1) | copy-done | bytes 917528
  62.8 0.0 copy-start.2
  62.8 1.1 %copy-done.2 = bf16[288,4,256]{2,1,0:T(4,128)(2,1)S(1)} copy-done((bf16[288,4,256]{2,1,0:T(4,128)(2,1)S(1)}, bf16[288,4,256]{2,1,0:T(4,128)(2,1)}, u32[]{:S(2)}) %copy-start.2) | copy-done | bytes 589848
  63.8 0.0 copy-start.3
  63.8 1.0 %copy-done.3 = bf16[2,1024,128]{2,1,0:T(8,128)(2,1)S(1)} copy-done((bf16[2,1024,128]{2,1,0:T(8,128)(2,1)S(1)}, bf16[2,1024,128]{2,1,0:T(8,128)(2,1)}, u32[]{:S(2)}) %copy-start.3) | copy-done | bytes 524312
  64.9 2.8 %shard_map.94 = (bf16[288,4,256]{2,1,0:T(4,128)(2,1)}, bf16[5120,128]{1,0:T(8,128)(2,1)}, f32[1024,256]{1,0:T(8,128)}, f32[1792,256]{1,0:T(8,128)}) custom-call(bf16[288,4,256]{2,1,0:T(4,128)(2,1)S(1)} %copy-done.2, bf16[5120,128]{1,0:T(8,128)(2,1)S(1)} %copy-done, bf16[2,1792,128]{2,1,0:T(8,128)(2,1)S(1)} %copy-done.1, bf16[2,1024,128]{2,1,0:T(8,128)(2,1)S(1)} %copy-done.3), custom_call_target="tpu_custom_call" | custom-call | tf_op jit(solution)/shard_map/pallas_call | solution.py:520
Async XLA Ops:
  60.3 1.3 %copy-start = (bf16[5120,128]{1,0:T(8,128)(2,1)S(1)}, bf16[5120,128]{1,0:T(8,128)(2,1)}, u32[]{:S(2)}) copy-start(bf16[5120,128]{1,0:T(8,128)(2,1)} %get-tuple-element.13.fineg_h) | copy-start | bytes 3932164
  61.6 1.2 %copy-start.1 = (bf16[2,1792,128]{2,1,0:T(8,128)(2,1)S(1)}, bf16[2,1792,128]{2,1,0:T(8,128)(2,1)}, u32[]{:S(2)}) copy-start(bf16[2,1792,128]{2,1,0:T(8,128)(2,1)} %get-tuple-element.14.ga) | copy-start | bytes 2752516
  62.8 1.1 %copy-start.2 = (bf16[288,4,256]{2,1,0:T(4,128)(2,1)S(1)}, bf16[288,4,256]{2,1,0:T(4,128)(2,1)}, u32[]{:S(2)}) copy-start(bf16[288,4,256]{2,1,0:T(4,128)(2,1)} %get-tuple-element.12.coarse_h) | copy-start | bytes 1769476
  63.8 1.0 %copy-start.3 = (bf16[2,1024,128]{2,1,0:T(8,128)(2,1)S(1)}, bf16[2,1024,128]{2,1,0:T(8,128)(2,1)}, u32[]{:S(2)}) copy-start(bf16[2,1024,128]{2,1,0:T(8,128)(2,1)} %get-tuple-element.15.gd) | copy-start | bytes 1572868

commit v3 on v2

--- a/solution.py
+++ b/solution.py
@@ -77,9 +77,9 @@
         ext[1 + q, 1:5, BP * z:BP * (z + 1), :] = rows.reshape(4, BP, 256)
 
 
-def kernel(fine_h, tgt, nb, wd_h, wc_h, cot_h,
-           coarse_h, fineg_h, ga, gd,
-           fin, cin, wd, wc, wt, t_scr, n_scr, wide, tall, fine, coarse_v, fineg_v,
+def kernel(fine_h, tgt_h, nb_h, wd_h, wc_h, cot_h,
+           coarse_h, fineg_h, ga_h, gd_h,
+           tgt, nb, ga, gd, fin, cin, wd, wc, wt, t_scr, n_scr, wide, tall, fine, coarse_v, fineg_v,
            cotx, hidx, gh, red, slope, fine_t, hid_t, gr, selc, selp,
            osnd, orcv, rsnd, rrcv, fsnd, frcv, hsnd, hrcv,
            pa, pd, ca, cd, qa, qd, xa, xd, za, ya, yd, wa,
@@ -99,7 +99,7 @@
         pl.semaphore_signal(barrier, inc=1, device_id=peer, device_id_type=MESH)
 
     loads = [pltpu.make_async_copy(src, dst, isem.at[i]) for i, (src, dst) in enumerate(
-        ((cot_h, cin), (fine_h, fin), (wd_h, wd), (wc_h, wc)))]
+        ((cot_h, cin), (fine_h, fin), (wd_h, wd), (wc_h, wc), (nb_h, nb), (tgt_h, tgt)))]
     for c in loads:
         c.start()
 
@@ -111,6 +111,7 @@
     quad_c = lax.shift_right_arithmetic(iota((128, 128), 0), 5)
     lane = iota((128, 128), 1)
 
+    loads[4].wait()
     n_scr[...] = jnp.full((8, 128), -1, I32)
     for q in range(4):
         n_scr[0:6, BP * q:BP * q + MB] = nb[...]
@@ -181,6 +182,7 @@
         flat = (sx + 1) * 3 + (sy + 1)
         return cell, moving, jnp.where(flat > 4, flat - 1, flat)
 
+    loads[5].wait()
     t_scr[:, 0:NB] = jnp.broadcast_to(tgt[...], (128, NB))
     cell_c, moving_c, dest_c = place(t_scr[...].T[0:NB, 0:1])
     cell_r, moving_r, dest_r = place(tgt[...])
@@ -234,13 +236,6 @@
         wt[d * 256:(d + 1) * 256, :] = wc[d * 256:(d + 1) * 256, :].T
     take_faces(cotx, frcv, cot_faces)
 
-    def back_conv(x, carry):
-        rows = jnp.concatenate([view(cotx, x, OPP[d]) for d in range(7)], axis=1)
-        gh[x] = dot(rows, wt[...]).astype(BF)
-        return carry
-
-    lax.fori_loop(0, 4, back_conv, 0)
-
     for c in octs:
         c.wait_recv()
     tag = orcv[:, 64:80, :].reshape(128, 256).astype(F32)
@@ -249,22 +244,6 @@
     came = [jnp.where(match & (row_half == h), 1.0, 0.0) for h in range(2)]
     came_t = [m.T.astype(BF) for m in came]
     came = [m.astype(BF) for m in came]
-
-    def grads(c):
-        i, j, k = c >> 2, (c >> 1) & 1, c & 1
-        out = []
-        for o in range(8):
-            x, y, z = 2 * (o >> 2) + i, 2 * ((o >> 1) & 1) + j, 2 * (o & 1) + k
-            out.append(gh[x, (y * 4 + z) * BP:(y * 4 + z + 1) * BP, :])
-        return jnp.concatenate(out, axis=0)
-
-    for pair in range(4):
-        out = (dot(came[0], grads(2 * pair)) + dot(came[1], grads(2 * pair + 1))).astype(BF)
-        for d in range(8):
-            rsnd[d, pair * 16:(pair + 1) * 16, :] = out[d * 16:(d + 1) * 16]
-    rets = [remote(rsnd.at[d], rrcv.at[d], rsem, d, at(-DIRS[d][0], -DIRS[d][1])) for d in range(8)]
-    for c in rets:
-        c.start()
 
     for c in range(8):
         i, j, k = c >> 2, (c >> 1) & 1, c & 1
@@ -286,6 +265,125 @@
             pa[h, d * 256:(d + 1) * 256, :] = acc[:, h * 128:(h + 1) * 128]
     core_a = remote(pa.at[1 - gz], ca, coresem, 0, other)
     core_a.start()
+
+    def x_start(core, p, cbuf, q, xbuf, n, s):
+        core.wait_recv()
+        q[...] = (p[gz].astype(F32) + cbuf[...].astype(F32)).astype(BF)
+        copies = []
+        for k in range(1, NX):
+            to = at(k, 0)
+            copies.append(remote(q.at[pl.ds(pl.multiple_of(to[0] * n, 16), n)], xbuf.at[k], xsem, s * NX + k, to))
+        for c in copies:
+            c.start()
+        return copies
+
+    def z_start(copies, q, xbuf, zbuf, ybuf, n, s):
+        for c in copies:
+            c.wait_recv()
+        acc = q[pl.ds(pl.multiple_of(gx * n, 16), n), :].astype(F32)
+        for k in range(1, NX):
+            acc = acc + xbuf[k].astype(F32)
+        units = n // 16
+        zbuf[0:units] = acc.astype(BF).reshape(units, 16, 128)
+        zbuf[units:8] = jnp.zeros((8 - units, 16, 128), BF)
+        out = []
+        for k in range(1, NY):
+            to = at(0, k)
+            out.append(remote(zbuf.at[to[1]], ybuf.at[k], zsem, s * NY + k, to))
+        for c in out:
+            c.start()
+        return out
+
+    def zg_start(copies, zbuf, ybuf, wbuf, s):
+        for c in copies:
+            c.wait_recv()
+        acc = zbuf[gy].astype(F32)
+        for k in range(1, NY):
+            acc = acc + ybuf[k].astype(F32)
+        wbuf[gy] = acc.astype(BF)
+        out = [remote(wbuf.at[gy], wbuf.at[gy], zgsem, s * NY + k, at(0, k)) for k in range(1, NY)]
+        for c in out:
+            c.start()
+        return out
+
+    def xg_start(copies, wbuf, g, n, s):
+        for c in copies:
+            c.wait_recv()
+        mine = pl.ds(pl.multiple_of(gx * n, 16), n)
+        g[gz, mine, :] = wbuf[0:n // 16].reshape(n, 128)
+        out = [remote(g.at[gz, mine], g.at[gz, mine], xgsem, s * NX + k, at(k, 0)) for k in range(1, NX)]
+        for c in out:
+            c.start()
+        return out
+
+    def cg_start(copies, g, s):
+        for c in copies:
+            c.wait_recv()
+        out = remote(g.at[gz], g.at[gz], cgsem, s, other)
+        out.start()
+        return out
+
+    def zb_start(copies, q, xbuf, ybuf, n, s):
+        for c in copies:
+            c.wait_recv()
+        acc = q[pl.ds(pl.multiple_of(gx * n, 16), n), :].astype(F32)
+        for k in range(1, NX):
+            acc = acc + xbuf[k].astype(F32)
+        ybuf[gy] = acc.astype(BF)
+        out = [remote(ybuf.at[gy], ybuf.at[gy], zsem, s * NY + k, at(0, k)) for k in range(1, NY)]
+        for c in out:
+            c.start()
+        return out
+
+    def xb_start(copies, ybuf, g, n, s):
+        for c in copies:
+            c.wait_recv()
+        acc = ybuf[0].astype(F32)
+        for k in range(1, NY):
+            acc = acc + ybuf[k].astype(F32)
+        mine = pl.ds(pl.multiple_of(gx * n, 16), n)
+        g[gz, mine, :] = acc.astype(BF)
+        out = [remote(g.at[gz, mine], g.at[gz, mine], xgsem, s * NX + k, at(k, 0)) for k in range(1, NX)]
+        for c in out:
+            c.start()
+        return out
+
+    def back_conv(x, carry):
+        rows = jnp.concatenate([view(cotx, x, OPP[d]) for d in range(7)], axis=1)
+        gh[x] = dot(rows, wt[...]).astype(BF)
+        return carry
+
+    lax.fori_loop(0, 3, back_conv, 0)
+    xs_a = x_start(core_a, pa, ca, qa, xa, KA, 0)
+    lax.fori_loop(3, 4, back_conv, 0)
+
+    def grads(c):
+        i, j, k = c >> 2, (c >> 1) & 1, c & 1
+        out = []
+        for o in range(8):
+            x, y, z = 2 * (o >> 2) + i, 2 * ((o >> 1) & 1) + j, 2 * (o & 1) + k
+            out.append(gh[x, (y * 4 + z) * BP:(y * 4 + z + 1) * BP, :])
+        return jnp.concatenate(out, axis=0)
+
+    for pair in range(4):
+        out = (dot(came[0], grads(2 * pair)) + dot(came[1], grads(2 * pair + 1))).astype(BF)
+        for d in range(8):
+            rsnd[d, pair * 16:(pair + 1) * 16, :] = out[d * 16:(d + 1) * 16]
+    rets = [remote(rsnd.at[d], rrcv.at[d], rsem, d, at(-DIRS[d][0], -DIRS[d][1])) for d in range(8)]
+    for c in rets:
+        c.start()
+
+    take_faces(hidx, hrcv, hid_faces)
+
+    def conv(x, carry):
+        rows = jnp.concatenate([view(hidx, x, d) for d in range(7)], axis=1)
+        acc = dot(rows, wc[...])
+        for p in range(16):
+            for h in range(2):
+                tall[h, pl.ds(x * 16 + p, BP, stride=64), :] = acc[p * BP:(p + 1) * BP, h * 128:(h + 1) * 128]
+        return carry
+
+    lax.fori_loop(0, 2, conv, 0)
 
     for c in rets:
         c.wait_recv()
@@ -300,112 +398,15 @@
     core_d = remote(pd.at[1 - gz], cd, coresem, 1, other)
     core_d.start()
 
-    def x_start(core, p, cbuf, q, xbuf, n, s):
-        core.wait_recv()
-        q[...] = (p[gz].astype(F32) + cbuf[...].astype(F32)).astype(BF)
-        copies = []
-        for k in range(1, NX):
-            to = at(k, 0)
-            copies.append(remote(q.at[pl.ds(pl.multiple_of(to[0] * n, 16), n)], xbuf.at[k], xsem, s * NX + k, to))
-        for c in copies:
-            c.start()
-        return copies
-
-    def z_start(copies, q, xbuf, zbuf, ybuf, n, s):
-        for c in copies:
-            c.wait_recv()
-        acc = q[pl.ds(pl.multiple_of(gx * n, 16), n), :].astype(F32)
-        for k in range(1, NX):
-            acc = acc + xbuf[k].astype(F32)
-        units = n // 16
-        zbuf[0:units] = acc.astype(BF).reshape(units, 16, 128)
-        zbuf[units:8] = jnp.zeros((8 - units, 16, 128), BF)
-        out = []
-        for k in range(1, NY):
-            to = at(0, k)
-            out.append(remote(zbuf.at[to[1]], ybuf.at[k], zsem, s * NY + k, to))
-        for c in out:
-            c.start()
-        return out
-
-    def zg_start(copies, zbuf, ybuf, wbuf, s):
-        for c in copies:
-            c.wait_recv()
-        acc = zbuf[gy].astype(F32)
-        for k in range(1, NY):
-            acc = acc + ybuf[k].astype(F32)
-        wbuf[gy] = acc.astype(BF)
-        out = [remote(wbuf.at[gy], wbuf.at[gy], zgsem, s * NY + k, at(0, k)) for k in range(1, NY)]
-        for c in out:
-            c.start()
-        return out
-
-    def xg_start(copies, wbuf, g, n, s):
-        for c in copies:
-            c.wait_recv()
-        mine = pl.ds(pl.multiple_of(gx * n, 16), n)
-        g[gz, mine, :] = wbuf[0:n // 16].reshape(n, 128)
-        out = [remote(g.at[gz, mine], g.at[gz, mine], xgsem, s * NX + k, at(k, 0)) for k in range(1, NX)]
-        for c in out:
-            c.start()
-        return out
-
-    def cg_start(copies, g, s):
-        for c in copies:
-            c.wait_recv()
-        out = remote(g.at[gz], g.at[gz], cgsem, s, other)
-        out.start()
-        return out
-
-    def zb_start(copies, q, xbuf, ybuf, n, s):
-        for c in copies:
-            c.wait_recv()
-        acc = q[pl.ds(pl.multiple_of(gx * n, 16), n), :].astype(F32)
-        for k in range(1, NX):
-            acc = acc + xbuf[k].astype(F32)
-        ybuf[gy] = acc.astype(BF)
-        out = [remote(ybuf.at[gy], ybuf.at[gy], zsem, s * NY + k, at(0, k)) for k in range(1, NY)]
-        for c in out:
-            c.start()
-        return out
-
-    def xb_start(copies, ybuf, g, n, s):
-        for c in copies:
-            c.wait_recv()
-        acc = ybuf[0].astype(F32)
-        for k in range(1, NY):
-            acc = acc + ybuf[k].astype(F32)
-        mine = pl.ds(pl.multiple_of(gx * n, 16), n)
-        g[gz, mine, :] = acc.astype(BF)
-        out = [remote(g.at[gz, mine], g.at[gz, mine], xgsem, s * NX + k, at(k, 0)) for k in range(1, NX)]
-        for c in out:
-            c.start()
-        return out
-
-    xs_a = x_start(core_a, pa, ca, qa, xa, KA, 0)
+    lax.fori_loop(2, 4, conv, 0)
     xs_d = x_start(core_d, pd, cd, qd, xd, KD, 1)
-
-    take_faces(hidx, hrcv, hid_faces)
-
-    def conv(x, carry):
-        rows = jnp.concatenate([view(hidx, x, d) for d in range(7)], axis=1)
-        acc = dot(rows, wc[...])
-        for p in range(16):
-            for h in range(2):
-                tall[h, pl.ds(x * 16 + p, BP, stride=64), :] = acc[p * BP:(p + 1) * BP, h * 128:(h + 1) * 128]
-        return carry
-
-    lax.fori_loop(0, 4, conv, 0)
+    zs_a = z_start(xs_a, qa, xa, za, ya, KA, 0)
     for m in range(16 * MB):
         for h in range(2):
             coarse_v[m, :, h * 128:(h + 1) * 128] = tall[h, 4 * m:4 * m + 4, :].astype(BF)
     stores = [pltpu.make_async_copy(coarse_v, coarse_h, esem.at[0])]
     stores[0].start()
-
-    zs_a = z_start(xs_a, qa, xa, za, ya, KA, 0)
-    zs_d = zb_start(xs_d, qd, xd, yd, KD, 1)
     zg_a = zg_start(zs_a, za, ya, wa, 0)
-    xg_d = xb_start(zs_d, yd, gd, KD, 1)
 
     for c in range(8):
         flow = dot_nt(gr[c * NB:(c + 1) * NB, :], wd[...])
@@ -415,11 +416,21 @@
     stores.append(pltpu.make_async_copy(fineg_v, fineg_h, esem.at[1]))
     stores[1].start()
 
+    zs_d = zb_start(xs_d, qd, xd, yd, KD, 1)
     xg_a = xg_start(zg_a, wa, ga, KA, 0)
+    xg_d = xb_start(zs_d, yd, gd, KD, 1)
+    cg_a = cg_start(xg_a, ga, 0)
+    stores.append(pltpu.make_async_copy(ga.at[gz], ga_h.at[gz], esem.at[2]))
+    stores[2].start()
     cg_d = cg_start(xg_d, gd, 1)
-    cg_a = cg_start(xg_a, ga, 0)
+    stores.append(pltpu.make_async_copy(gd.at[gz], gd_h.at[gz], esem.at[3]))
+    stores[3].start()
+    cg_a.wait_recv()
+    stores.append(pltpu.make_async_copy(ga.at[1 - gz], ga_h.at[1 - gz], esem.at[4]))
+    stores[4].start()
     cg_d.wait_recv()
-    cg_a.wait_recv()
+    stores.append(pltpu.make_async_copy(gd.at[1 - gz], gd_h.at[1 - gz], esem.at[5]))
+    stores[5].start()
     for c in stores:
         c.wait()
 
@@ -428,21 +439,35 @@
         c.wait_send()
 
 
-def finish(coarse_h, fineg_h, ga, gd, coarse_o, fineg_o, down_o, conv_o, sem):
-    copies = [pltpu.make_async_copy(coarse_h, coarse_o, sem.at[0]),
-              pltpu.make_async_copy(fineg_h, fineg_o, sem.at[1])]
-    for c in copies:
+def finish(coarse_h, fineg_h, ga_h, gd_h, coarse_o, fineg_o, down_h, conv_h,
+           coarse, fineg, ga, gd, down, conv, sem):
+    reads = [pltpu.make_async_copy(src, dst, sem.at[i]) for i, (src, dst) in enumerate(
+        ((gd_h, gd), (ga_h, ga), (fineg_h, fineg), (coarse_h, coarse)))]
+    for c in reads:
         c.start()
+    writes = [pltpu.make_async_copy(src, dst, sem.at[4 + i]) for i, (src, dst) in enumerate(
+        ((down, down_h), (fineg, fineg_o), (coarse, coarse_o)))]
     scale = 1.0 / (64 * MB)
+    reads[0].wait()
     for h in range(2):
-        down_o[:, h * 128:(h + 1) * 128] = gd[h].astype(F32) * scale
-        conv_o[:, h * 128:(h + 1) * 128] = ga[h].astype(F32) * scale
-    for c in copies:
+        down[:, h * 128:(h + 1) * 128] = gd[h].astype(F32) * scale
+    writes[0].start()
+    reads[1].wait()
+    for m in range(7):
+        rows = slice(m * 256, (m + 1) * 256)
+        for h in range(2):
+            conv[rows, h * 128:(h + 1) * 128] = ga[h, rows].astype(F32) * scale
+        writes.append(pltpu.make_async_copy(conv.at[rows], conv_h.at[rows], sem.at[7 + m]))
+        writes[3 + m].start()
+    reads[2].wait()
+    writes[1].start()
+    reads[3].wait()
+    writes[2].start()
+    for c in writes:
         c.wait()
 
 
 def shards(fine_field, target, neighbour, down_weight, conv_weight, out_cotangent):
-    vmem = pl.BlockSpec(memory_space=pltpu.VMEM)
     anyw = pl.BlockSpec(memory_space=pl.ANY)
     dma = pltpu.SemaphoreType.DMA
     coarse, fineg, ga, gd = pl.pallas_call(
@@ -453,9 +478,13 @@
             jax.ShapeDtypeStruct((2, 1792, 128), BF),
             jax.ShapeDtypeStruct((2, 1024, 128), BF),
         ),
-        in_specs=[anyw, vmem, vmem, anyw, anyw, anyw],
-        out_specs=[anyw, anyw, vmem, vmem],
+        in_specs=[anyw] * 6,
+        out_specs=[anyw] * 4,
         scratch_shapes=[
+            pltpu.VMEM((1, NB), I32),
+            pltpu.VMEM((6, MB), I32),
+            pltpu.VMEM((2, 1792, 128), BF),
+            pltpu.VMEM((2, 1024, 128), BF),
             pltpu.VMEM((64 * NB, 128), BF),
             pltpu.VMEM((16 * MB, 4, 256), BF),
             pltpu.VMEM((1024, 256), BF),
@@ -498,8 +527,8 @@
             pltpu.VMEM((NY, 16, 128), BF),
             pltpu.VMEM((NY, KD, 128), BF),
             pltpu.VMEM((NY, 16, 128), BF),
-            dma((4,)),
-            dma((2,)),
+            dma((6,)),
+            dma((6,)),
             dma((2, 8)),
             dma((2, 8)),
             dma((2, 5)),
@@ -525,10 +554,18 @@
             jax.ShapeDtypeStruct((1024, 256), F32),
             jax.ShapeDtypeStruct((1792, 256), F32),
         ),
-        in_specs=[anyw, anyw, vmem, vmem],
-        out_specs=[anyw, anyw, vmem, vmem],
-        scratch_shapes=[dma((2,))],
-        compiler_params=pltpu.CompilerParams(vmem_limit_bytes=32 * 1024 * 1024),
+        in_specs=[anyw] * 4,
+        out_specs=[anyw] * 4,
+        scratch_shapes=[
+            pltpu.VMEM((16 * MB, 4, 256), BF),
+            pltpu.VMEM((64 * NB, 128), BF),
+            pltpu.VMEM((2, 1792, 128), BF),
+            pltpu.VMEM((2, 1024, 128), BF),
+            pltpu.VMEM((1024, 256), F32),
+            pltpu.VMEM((1792, 256), F32),
+            dma((14,)),
+        ],
+        compiler_params=pltpu.CompilerParams(vmem_limit_bytes=60 * 1024 * 1024),
     )(coarse, fineg, ga, gd)
     return (coarse.reshape(MB, 4, 4, 4, 256), fineg.reshape(NB, 8, 8, 128), down_g,
             conv_g.reshape(7, 256, 256))

time: 68.2 us -> 68.6 us (level)
  Pallas kernels: 62.5 us -> 67.7 us
  local copies, waits for them, and re-layouts: 4.59 us -> 0 us
    pallas_call x1, Pallas kernels: 59.6 us -> 64.2 us  [shards(): pl.pallas_call(kernel, out_shape=(jax.ShapeDtypeStruct((16 * MB, 4, 256),...]
    unnamed x8 -> x0, local copies, waits for them, and re-layouts: 4.59 us -> none
where the time goes in v3:
time: 68.6 us; the launch traced here: 68.5 us
  Pallas kernels  67.7 us (99%)
  between operations  0.8 us (1%)
    pallas_call x1, Pallas kernels, shards(): pl.pallas_call(kernel, out_shape=(jax.ShapeDtypeStruct((16 * MB, 4, 256),...  64.2 us
    pallas_call x1, Pallas kernels, shards(): pl.pallas_call(finish, out_shape=(jax.ShapeDtypeStruct((16 * MB, 4, 256),...  3.45 us

profile of v3, /device:TPU:1, one launch (start us, length us, event | category | flops | bytes accessed | tf_op | source)
XLA Modules:
  0.0 68.5 jit_solution(5979940594613675398)
XLA Ops:
  0.6 64.2 %shard_map.93 = (bf16[288,4,256]{2,1,0:T(4,128)(2,1)}, bf16[5120,128]{1,0:T(8,128)(2,1)}, bf16[2,1792,128]{2,1,0:T(8,128)(2,1)}, bf16[2,1024,128]{2,1,0:T(8,128)(2,1)}) custom-call(bf16[5120,128]{1,0:T(8,128)(2,1)} %bitcast.9, s32[1,80]{1,0:T(1,128)} %bitcast.15, s32[6,18]{1,0:T(8,128)} %bitcast.14, bf16[1024,256]{1,0:T(8,128)(2,1)} %wd_h.1, ...), custom_call_target="tpu_custom_call" | custom-call | flops 6000000000 | bytes 10000000 | tf_op jit(solution)/shard_map/pallas_call | solution.py:473
  64.9 3.4 %shard_map.94 = (bf16[288,4,256]{2,1,0:T(4,128)(2,1)}, bf16[5120,128]{1,0:T(8,128)(2,1)}, f32[1024,256]{1,0:T(8,128)}, f32[1792,256]{1,0:T(8,128)}) custom-call(bf16[288,4,256]{2,1,0:T(4,128)(2,1)} %get-tuple-element.12.coarse_h, bf16[5120,128]{1,0:T(8,128)(2,1)} %get-tuple-element.13.fineg_h, bf16[2,1792,128]{2,1,0:T(8,128)(2,1)} %get-tuple-element.14.ga_h, ...), custom_call_target="tpu_custom_call" | custom-call | tf_op jit(solution)/shard_map/pallas_call | solution.py:549

commit v4 on v3

--- a/solution.py
+++ b/solution.py
@@ -236,6 +236,13 @@
         wt[d * 256:(d + 1) * 256, :] = wc[d * 256:(d + 1) * 256, :].T
     take_faces(cotx, frcv, cot_faces)
 
+    def back_conv(x, carry):
+        rows = jnp.concatenate([view(cotx, x, OPP[d]) for d in range(7)], axis=1)
+        gh[x] = dot(rows, wt[...]).astype(BF)
+        return carry
+
+    lax.fori_loop(0, 4, back_conv, 0)
+
     for c in octs:
         c.wait_recv()
     tag = orcv[:, 64:80, :].reshape(128, 256).astype(F32)
@@ -244,6 +251,22 @@
     came = [jnp.where(match & (row_half == h), 1.0, 0.0) for h in range(2)]
     came_t = [m.T.astype(BF) for m in came]
     came = [m.astype(BF) for m in came]
+
+    def grads(c):
+        i, j, k = c >> 2, (c >> 1) & 1, c & 1
+        out = []
+        for o in range(8):
+            x, y, z = 2 * (o >> 2) + i, 2 * ((o >> 1) & 1) + j, 2 * (o & 1) + k
+            out.append(gh[x, (y * 4 + z) * BP:(y * 4 + z + 1) * BP, :])
+        return jnp.concatenate(out, axis=0)
+
+    for pair in range(4):
+        out = (dot(came[0], grads(2 * pair)) + dot(came[1], grads(2 * pair + 1))).astype(BF)
+        for d in range(8):
+            rsnd[d, pair * 16:(pair + 1) * 16, :] = out[d * 16:(d + 1) * 16]
+    rets = [remote(rsnd.at[d], rrcv.at[d], rsem, d, at(-DIRS[d][0], -DIRS[d][1])) for d in range(8)]
+    for c in rets:
+        c.start()
 
     for c in range(8):
         i, j, k = c >> 2, (c >> 1) & 1, c & 1
@@ -256,35 +279,47 @@
             hidx[1 + x, 1 + y, BP * (1 + z):BP * (2 + z), :] = hid[o * BP:(o + 1) * BP]
     hid_faces = send_faces(hidx, hsnd, hrcv, hsem)
 
-    for x in range(4):
-        hid_t[:, x * 512:(x + 1) * 512] = view(hidx, x, 0).T
-    for d in range(7):
-        rows = jnp.concatenate([view(cotx, x, OPP[d]) for x in range(4)], axis=0)
-        acc = dot(hid_t[...], rows).astype(BF)
-        for h in range(2):
-            pa[h, d * 256:(d + 1) * 256, :] = acc[:, h * 128:(h + 1) * 128]
-    core_a = remote(pa.at[1 - gz], ca, coresem, 0, other)
-    core_a.start()
-
-    def x_start(core, p, cbuf, q, xbuf, n, s):
+    def core_send(p, cbuf, m, s):
+        rows = pl.ds(m * 256, 256)
+        c = remote(p.at[1 - gz, rows], cbuf.at[rows], coresem, 7 * s + m, other)
+        c.start()
+        return c
+
+    def x_copy(src, dst, sems, s, p):
+        return pltpu.make_async_remote_copy(
+            src_ref=src, dst_ref=dst, send_sem=sems.at[0, s * NX + p], recv_sem=sems.at[1, s * NX + gx],
+            device_id=(p, gy, gz), device_id_type=MESH)
+
+    def x_from(dst, sems, s, p):
+        return pltpu.make_async_remote_copy(
+            src_ref=dst, dst_ref=dst, send_sem=sems.at[0, s * NX + p], recv_sem=sems.at[1, s * NX + p],
+            device_id=(p, gy, gz), device_id_type=MESH)
+
+    def away(p, fn):
+        @pl.when(gx != p)
+        def _():
+            fn()
+
+    def core_take(core, p, cbuf, q, xbuf, n, m, s):
         core.wait_recv()
-        q[...] = (p[gz].astype(F32) + cbuf[...].astype(F32)).astype(BF)
-        copies = []
-        for k in range(1, NX):
-            to = at(k, 0)
-            copies.append(remote(q.at[pl.ds(pl.multiple_of(to[0] * n, 16), n)], xbuf.at[k], xsem, s * NX + k, to))
-        for c in copies:
-            c.start()
-        return copies
-
-    def z_start(copies, q, xbuf, zbuf, ybuf, n, s):
-        for c in copies:
-            c.wait_recv()
-        acc = q[pl.ds(pl.multiple_of(gx * n, 16), n), :].astype(F32)
-        for k in range(1, NX):
-            acc = acc + xbuf[k].astype(F32)
+        rows = slice(m * 256, (m + 1) * 256)
+        q[rows] = (p[gz, rows].astype(F32) + cbuf[rows].astype(F32)).astype(BF)
+        for j in range(NX):
+            if m * 256 < (j + 1) * n <= (m + 1) * 256:
+                away(j, lambda j=j: x_copy(q.at[pl.ds(j * n, n)], xbuf.at[gx], xsem, s, j).start())
+
+    def x_sum(q, xbuf, n, s):
+        xbuf[gx] = q[pl.ds(pl.multiple_of(gx * n, 16), n), :]
+        for j in range(NX):
+            away(j, lambda j=j: x_from(xbuf.at[j], xsem, s, j).wait_recv())
+        acc = xbuf[0].astype(F32)
+        for j in range(1, NX):
+            acc = acc + xbuf[j].astype(F32)
+        return acc.astype(BF)
+
+    def z_start(acc, zbuf, ybuf, n, s):
         units = n // 16
-        zbuf[0:units] = acc.astype(BF).reshape(units, 16, 128)
+        zbuf[0:units] = acc.reshape(units, 16, 128)
         zbuf[units:8] = jnp.zeros((8 - units, 16, 128), BF)
         out = []
         for k in range(1, NY):
@@ -306,74 +341,72 @@
             c.start()
         return out
 
-    def xg_start(copies, wbuf, g, n, s):
-        for c in copies:
-            c.wait_recv()
-        mine = pl.ds(pl.multiple_of(gx * n, 16), n)
-        g[gz, mine, :] = wbuf[0:n // 16].reshape(n, 128)
-        out = [remote(g.at[gz, mine], g.at[gz, mine], xgsem, s * NX + k, at(k, 0)) for k in range(1, NX)]
-        for c in out:
-            c.start()
-        return out
-
-    def cg_start(copies, g, s):
-        for c in copies:
-            c.wait_recv()
-        out = remote(g.at[gz], g.at[gz], cgsem, s, other)
-        out.start()
-        return out
-
-    def zb_start(copies, q, xbuf, ybuf, n, s):
-        for c in copies:
-            c.wait_recv()
-        acc = q[pl.ds(pl.multiple_of(gx * n, 16), n), :].astype(F32)
-        for k in range(1, NX):
-            acc = acc + xbuf[k].astype(F32)
-        ybuf[gy] = acc.astype(BF)
+    def zb_start(acc, ybuf, s):
+        ybuf[gy] = acc
         out = [remote(ybuf.at[gy], ybuf.at[gy], zsem, s * NY + k, at(0, k)) for k in range(1, NY)]
         for c in out:
             c.start()
         return out
 
-    def xb_start(copies, ybuf, g, n, s):
+    def xg_start(rows, g, n, s):
+        mine = pl.ds(pl.multiple_of(gx * n, 16), n)
+        g[gz, mine, :] = rows
+        for j in range(NX):
+            away(j, lambda j=j: x_copy(g.at[gz, mine], g.at[gz, mine], xgsem, s, j).start())
+
+    def gathered_w(copies, wbuf, n):
+        for c in copies:
+            c.wait_recv()
+        return wbuf[0:n // 16].reshape(n, 128)
+
+    def gathered_y(copies, ybuf):
         for c in copies:
             c.wait_recv()
         acc = ybuf[0].astype(F32)
         for k in range(1, NY):
             acc = acc + ybuf[k].astype(F32)
-        mine = pl.ds(pl.multiple_of(gx * n, 16), n)
-        g[gz, mine, :] = acc.astype(BF)
-        out = [remote(g.at[gz, mine], g.at[gz, mine], xgsem, s * NX + k, at(k, 0)) for k in range(1, NX)]
-        for c in out:
-            c.start()
+        return acc.astype(BF)
+
+    def cg_start(g, n, s):
+        out = []
+        for quarter in range(4):
+            for j in range(4 * quarter, 4 * quarter + 4):
+                away(j, lambda j=j: x_from(g.at[gz, pl.ds(j * n, n)], xgsem, s, j).wait_recv())
+            rows = pl.ds(4 * quarter * n, 4 * n)
+            out.append(remote(g.at[gz, rows], g.at[gz, rows], cgsem, 4 * s + quarter, other))
+            out[quarter].start()
         return out
 
-    def back_conv(x, carry):
-        rows = jnp.concatenate([view(cotx, x, OPP[d]) for d in range(7)], axis=1)
-        gh[x] = dot(rows, wt[...]).astype(BF)
-        return carry
-
-    lax.fori_loop(0, 3, back_conv, 0)
-    xs_a = x_start(core_a, pa, ca, qa, xa, KA, 0)
-    lax.fori_loop(3, 4, back_conv, 0)
-
-    def grads(c):
-        i, j, k = c >> 2, (c >> 1) & 1, c & 1
-        out = []
-        for o in range(8):
-            x, y, z = 2 * (o >> 2) + i, 2 * ((o >> 1) & 1) + j, 2 * (o & 1) + k
-            out.append(gh[x, (y * 4 + z) * BP:(y * 4 + z + 1) * BP, :])
-        return jnp.concatenate(out, axis=0)
-
-    for pair in range(4):
-        out = (dot(came[0], grads(2 * pair)) + dot(came[1], grads(2 * pair + 1))).astype(BF)
-        for d in range(8):
-            rsnd[d, pair * 16:(pair + 1) * 16, :] = out[d * 16:(d + 1) * 16]
-    rets = [remote(rsnd.at[d], rrcv.at[d], rsem, d, at(-DIRS[d][0], -DIRS[d][1])) for d in range(8)]
+    for x in range(4):
+        hid_t[:, x * 512:(x + 1) * 512] = view(hidx, x, 0).T
+    cores_a = []
+    for d in range(7):
+        rows = jnp.concatenate([view(cotx, x, OPP[d]) for x in range(4)], axis=0)
+        acc = dot(hid_t[...], rows).astype(BF)
+        for h in range(2):
+            pa[h, d * 256:(d + 1) * 256, :] = acc[:, h * 128:(h + 1) * 128]
+        cores_a.append(core_send(pa, ca, d, 0))
+        if d >= 5:
+            core_take(cores_a[d - 5], pa, ca, qa, xa, KA, d - 5, 0)
+    for d in range(2, 7):
+        core_take(cores_a[d], pa, ca, qa, xa, KA, d, 0)
+
     for c in rets:
-        c.start()
+        c.wait_recv()
+    for c in range(8):
+        back = rrcv[:, (c >> 1) * 16:(c >> 1) * 16 + 16, :].reshape(128, 256)
+        grad = dot(stay_c, grads(c)) + dot(back_hot[c & 1], back)
+        gr[c * NB:(c + 1) * NB, :] = (grad * slope[c * NB:(c + 1) * NB, :]).astype(BF)
+    cores_d = []
+    for m in range(4):
+        acc = dot(fine_t[m * 256:(m + 1) * 256, :], gr[...]).astype(BF)
+        for h in range(2):
+            pd[h, m * 256:(m + 1) * 256, :] = acc[:, h * 128:(h + 1) * 128]
+        cores_d.append(core_send(pd, cd, m, 1))
 
     take_faces(hidx, hrcv, hid_faces)
+    for m in range(4):
+        core_take(cores_d[m], pd, cd, qd, xd, KD, m, 1)
 
     def conv(x, carry):
         rows = jnp.concatenate([view(hidx, x, d) for d in range(7)], axis=1)
@@ -383,59 +416,52 @@
                 tall[h, pl.ds(x * 16 + p, BP, stride=64), :] = acc[p * BP:(p + 1) * BP, h * 128:(h + 1) * 128]
         return carry
 
-    lax.fori_loop(0, 2, conv, 0)
-
-    for c in rets:
-        c.wait_recv()
-    for c in range(8):
-        back = rrcv[:, (c >> 1) * 16:(c >> 1) * 16 + 16, :].reshape(128, 256)
-        grad = dot(stay_c, grads(c)) + dot(back_hot[c & 1], back)
-        gr[c * NB:(c + 1) * NB, :] = (grad * slope[c * NB:(c + 1) * NB, :]).astype(BF)
-    for m in range(4):
-        acc = dot(fine_t[m * 256:(m + 1) * 256, :], gr[...]).astype(BF)
-        for h in range(2):
-            pd[h, m * 256:(m + 1) * 256, :] = acc[:, h * 128:(h + 1) * 128]
-    core_d = remote(pd.at[1 - gz], cd, coresem, 1, other)
-    core_d.start()
-
-    lax.fori_loop(2, 4, conv, 0)
-    xs_d = x_start(core_d, pd, cd, qd, xd, KD, 1)
-    zs_a = z_start(xs_a, qa, xa, za, ya, KA, 0)
-    for m in range(16 * MB):
-        for h in range(2):
-            coarse_v[m, :, h * 128:(h + 1) * 128] = tall[h, 4 * m:4 * m + 4, :].astype(BF)
-    stores = [pltpu.make_async_copy(coarse_v, coarse_h, esem.at[0])]
-    stores[0].start()
-    zg_a = zg_start(zs_a, za, ya, wa, 0)
+    lax.fori_loop(0, 4, conv, 0)
+    zs_a = z_start(x_sum(qa, xa, KA, 0), za, ya, KA, 0)
+    zs_d = zb_start(x_sum(qd, xd, KD, 1), yd, 1)
 
     for c in range(8):
         flow = dot_nt(gr[c * NB:(c + 1) * NB, :], wd[...])
         for v in range(8):
             wide[pl.ds(c * 8 + v, NB, stride=64), :] = flow[:, v * 128:(v + 1) * 128]
     fineg_v[...] = wide[...].astype(BF)
-    stores.append(pltpu.make_async_copy(fineg_v, fineg_h, esem.at[1]))
+    stores = [pltpu.make_async_copy(fineg_v, fineg_h, esem.at[1])]
+    stores[0].start()
+    zg_a = zg_start(zs_a, za, ya, wa, 0)
+
+    for m in range(16 * MB):
+        for h in range(2):
+            coarse_v[m, :, h * 128:(h + 1) * 128] = tall[h, 4 * m:4 * m + 4, :].astype(BF)
+    stores.append(pltpu.make_async_copy(coarse_v, coarse_h, esem.at[0]))
     stores[1].start()
 
-    zs_d = zb_start(xs_d, qd, xd, yd, KD, 1)
-    xg_a = xg_start(zg_a, wa, ga, KA, 0)
-    xg_d = xb_start(zs_d, yd, gd, KD, 1)
-    cg_a = cg_start(xg_a, ga, 0)
+    xg_start(gathered_y(zs_d, yd), gd, KD, 1)
+    xg_start(gathered_w(zg_a, wa, KA), ga, KA, 0)
+    cg_d = cg_start(gd, KD, 1)
+    stores.append(pltpu.make_async_copy(gd.at[gz], gd_h.at[gz], esem.at[3]))
+    stores[2].start()
+    cg_a = cg_start(ga, KA, 0)
     stores.append(pltpu.make_async_copy(ga.at[gz], ga_h.at[gz], esem.at[2]))
-    stores[2].start()
-    cg_d = cg_start(xg_d, gd, 1)
-    stores.append(pltpu.make_async_copy(gd.at[gz], gd_h.at[gz], esem.at[3]))
     stores[3].start()
-    cg_a.wait_recv()
+    for c in cg_d:
+        c.wait_recv()
+    stores.append(pltpu.make_async_copy(gd.at[1 - gz], gd_h.at[1 - gz], esem.at[5]))
+    stores[4].start()
+    for c in cg_a:
+        c.wait_recv()
     stores.append(pltpu.make_async_copy(ga.at[1 - gz], ga_h.at[1 - gz], esem.at[4]))
-    stores[4].start()
-    cg_d.wait_recv()
-    stores.append(pltpu.make_async_copy(gd.at[1 - gz], gd_h.at[1 - gz], esem.at[5]))
     stores[5].start()
     for c in stores:
         c.wait()
-
-    for c in (octs + cot_faces + rets + hid_faces + [core_a, core_d] + xs_a + xs_d + zs_a + zs_d
-              + zg_a + xg_a + xg_d + [cg_a, cg_d]):
+    for j in range(NX):
+        def sent(j=j):
+            x_from(xa.at[j], xsem, 0, j).wait_send()
+            x_from(xd.at[j], xsem, 1, j).wait_send()
+            x_from(ga.at[gz, pl.ds(j * KA, KA)], xgsem, 0, j).wait_send()
+            x_from(gd.at[gz, pl.ds(j * KD, KD)], xgsem, 1, j).wait_send()
+
+        away(j, sent)
+    for c in (octs + cot_faces + rets + hid_faces + cores_a + cores_d + zs_a + zs_d + zg_a + cg_a + cg_d):
         c.wait_send()
 
 
@@ -533,12 +559,12 @@
             dma((2, 8)),
             dma((2, 5)),
             dma((2, 5)),
-            dma((2, 2)),
+            dma((2, 11)),
             dma((2, 2 * NX)),
             dma((2, 2 * NY)),
             dma((2, 2 * NY)),
             dma((2, 2 * NX)),
-            dma((2, 2)),
+            dma((2, 8)),
         ],
         compiler_params=pltpu.CompilerParams(
             collective_id=0, has_side_effects=True, vmem_limit_bytes=56 * 1024 * 1024),

time: 68.6 us -> 64.6 us (0.942)
  Pallas kernels: 67.7 us -> 63.6 us
    pallas_call x1, Pallas kernels: 64.2 us -> 60.2 us  [shards(): pl.pallas_call(kernel, out_shape=(jax.ShapeDtypeStruct((16 * MB, 4, 256),...]
where the time goes in v4:
time: 64.6 us; the launch traced here: 64.4 us
  Pallas kernels  63.6 us (98%)
  between operations  0.8 us (1%)
    pallas_call x1, Pallas kernels, shards(): pl.pallas_call(kernel, out_shape=(jax.ShapeDtypeStruct((16 * MB, 4, 256),...  60.2 us
    pallas_call x1, Pallas kernels, shards(): pl.pallas_call(finish, out_shape=(jax.ShapeDtypeStruct((16 * MB, 4, 256),...  3.45 us

profile of v4, /device:TPU:1, one launch (start us, length us, event | category | flops | bytes accessed | tf_op | source)
XLA Modules:
  0.0 64.4 jit_solution(11624644446230170690)
XLA Ops:
  0.6 60.2 %shard_map.93 = (bf16[288,4,256]{2,1,0:T(4,128)(2,1)}, bf16[5120,128]{1,0:T(8,128)(2,1)}, bf16[2,1792,128]{2,1,0:T(8,128)(2,1)}, bf16[2,1024,128]{2,1,0:T(8,128)(2,1)}) custom-call(bf16[5120,128]{1,0:T(8,128)(2,1)} %bitcast.9, s32[1,80]{1,0:T(1,128)} %bitcast.15, s32[6,18]{1,0:T(8,128)} %bitcast.14, bf16[1024,256]{1,0:T(8,128)(2,1)} %wd_h.1, ...), custom_call_target="tpu_custom_call" | custom-call | flops 6000000000 | bytes 10000000 | tf_op jit(solution)/shard_map/pallas_call | solution.py:499
  60.8 3.4 %shard_map.94 = (bf16[288,4,256]{2,1,0:T(4,128)(2,1)}, bf16[5120,128]{1,0:T(8,128)(2,1)}, f32[1024,256]{1,0:T(8,128)}, f32[1792,256]{1,0:T(8,128)}) custom-call(bf16[288,4,256]{2,1,0:T(4,128)(2,1)} %get-tuple-element.12.coarse_h, bf16[5120,128]{1,0:T(8,128)(2,1)} %get-tuple-element.13.fineg_h, bf16[2,1792,128]{2,1,0:T(8,128)(2,1)} %get-tuple-element.14.ga_h, ...), custom_call_target="tpu_custom_call" | custom-call | tf_op jit(solution)/shard_map/pallas_call | solution.py:575

commit v5 on v4

--- a/solution.py
+++ b/solution.py
@@ -82,8 +82,8 @@
            tgt, nb, ga, gd, fin, cin, wd, wc, wt, t_scr, n_scr, wide, tall, fine, coarse_v, fineg_v,
            cotx, hidx, gh, red, slope, fine_t, hid_t, gr, selc, selp,
            osnd, orcv, rsnd, rrcv, fsnd, frcv, hsnd, hrcv,
-           pa, pd, ca, cd, qa, qd, xa, xd, za, ya, yd, wa,
-           isem, esem, osem, rsem, fsem, hsem, coresem, xsem, zsem, zgsem, xgsem, cgsem):
+           pa, pd, ca, cd, qa, qd, xa, xd, ya, yd,
+           isem, esem, osem, rsem, fsem, hsem, coresem, xsem, zsem, xgsem, cgsem):
     gx, gy, gz = lax.axis_index("gx"), lax.axis_index("gy"), lax.axis_index("gz")
     myself = (gx * NY + gy) * NZ + gz
 
@@ -139,15 +139,15 @@
     face_to = (at(1, 0), at(-1, 0), at(0, 1), at(0, -1), other)
 
     def send_faces(ext, snd, rcv, sems):
+        copies = [remote(snd.at[k], rcv.at[k], sems, k, face_to[k]) for k in range(5)]
         for k in range(4):
             for q in range(4):
                 snd[k, q * 32:(q + 1) * 32, :] = dot(selc[OPP[k + 1] - 1], layer_quad(ext, k, q)).astype(BF)
+            copies[k].start()
         for q in range(4):
             both = dot(selc[5], layer_quad(ext, 4, q)) + dot(selc[4], layer_quad(ext, 5, q))
             snd[4, q * 32:(q + 1) * 32, :] = both.astype(BF)
-        copies = [remote(snd.at[k], rcv.at[k], sems, k, face_to[k]) for k in range(5)]
-        for c in copies:
-            c.start()
+        copies[4].start()
         return copies
 
     def take_faces(ext, rcv, copies):
@@ -236,12 +236,9 @@
         wt[d * 256:(d + 1) * 256, :] = wc[d * 256:(d + 1) * 256, :].T
     take_faces(cotx, frcv, cot_faces)
 
-    def back_conv(x, carry):
+    for x in range(4):
         rows = jnp.concatenate([view(cotx, x, OPP[d]) for d in range(7)], axis=1)
         gh[x] = dot(rows, wt[...]).astype(BF)
-        return carry
-
-    lax.fori_loop(0, 4, back_conv, 0)
 
     for c in octs:
         c.wait_recv()
@@ -317,30 +314,6 @@
             acc = acc + xbuf[j].astype(F32)
         return acc.astype(BF)
 
-    def z_start(acc, zbuf, ybuf, n, s):
-        units = n // 16
-        zbuf[0:units] = acc.reshape(units, 16, 128)
-        zbuf[units:8] = jnp.zeros((8 - units, 16, 128), BF)
-        out = []
-        for k in range(1, NY):
-            to = at(0, k)
-            out.append(remote(zbuf.at[to[1]], ybuf.at[k], zsem, s * NY + k, to))
-        for c in out:
-            c.start()
-        return out
-
-    def zg_start(copies, zbuf, ybuf, wbuf, s):
-        for c in copies:
-            c.wait_recv()
-        acc = zbuf[gy].astype(F32)
-        for k in range(1, NY):
-            acc = acc + ybuf[k].astype(F32)
-        wbuf[gy] = acc.astype(BF)
-        out = [remote(wbuf.at[gy], wbuf.at[gy], zgsem, s * NY + k, at(0, k)) for k in range(1, NY)]
-        for c in out:
-            c.start()
-        return out
-
     def zb_start(acc, ybuf, s):
         ybuf[gy] = acc
         out = [remote(ybuf.at[gy], ybuf.at[gy], zsem, s * NY + k, at(0, k)) for k in range(1, NY)]
@@ -353,11 +326,6 @@
         g[gz, mine, :] = rows
         for j in range(NX):
             away(j, lambda j=j: x_copy(g.at[gz, mine], g.at[gz, mine], xgsem, s, j).start())
-
-    def gathered_w(copies, wbuf, n):
-        for c in copies:
-            c.wait_recv()
-        return wbuf[0:n // 16].reshape(n, 128)
 
     def gathered_y(copies, ybuf):
         for c in copies:
@@ -408,16 +376,17 @@
     for m in range(4):
         core_take(cores_d[m], pd, cd, qd, xd, KD, m, 1)
 
-    def conv(x, carry):
+    def conv(x):
         rows = jnp.concatenate([view(hidx, x, d) for d in range(7)], axis=1)
         acc = dot(rows, wc[...])
         for p in range(16):
             for h in range(2):
                 tall[h, pl.ds(x * 16 + p, BP, stride=64), :] = acc[p * BP:(p + 1) * BP, h * 128:(h + 1) * 128]
-        return carry
-
-    lax.fori_loop(0, 4, conv, 0)
-    zs_a = z_start(x_sum(qa, xa, KA, 0), za, ya, KA, 0)
+
+    for x in range(3):
+        conv(x)
+    zs_a = zb_start(x_sum(qa, xa, KA, 0), ya, 0)
+    conv(3)
     zs_d = zb_start(x_sum(qd, xd, KD, 1), yd, 1)
 
     for c in range(8):
@@ -427,7 +396,6 @@
     fineg_v[...] = wide[...].astype(BF)
     stores = [pltpu.make_async_copy(fineg_v, fineg_h, esem.at[1])]
     stores[0].start()
-    zg_a = zg_start(zs_a, za, ya, wa, 0)
 
     for m in range(16 * MB):
         for h in range(2):
@@ -435,21 +403,21 @@
     stores.append(pltpu.make_async_copy(coarse_v, coarse_h, esem.at[0]))
     stores[1].start()
 
+    xg_start(gathered_y(zs_a, ya), ga, KA, 0)
     xg_start(gathered_y(zs_d, yd), gd, KD, 1)
-    xg_start(gathered_w(zg_a, wa, KA), ga, KA, 0)
+    cg_a = cg_start(ga, KA, 0)
+    stores.append(pltpu.make_async_copy(ga.at[gz], ga_h.at[gz], esem.at[2]))
+    stores[2].start()
     cg_d = cg_start(gd, KD, 1)
     stores.append(pltpu.make_async_copy(gd.at[gz], gd_h.at[gz], esem.at[3]))
-    stores[2].start()
-    cg_a = cg_start(ga, KA, 0)
-    stores.append(pltpu.make_async_copy(ga.at[gz], ga_h.at[gz], esem.at[2]))
     stores[3].start()
+    for c in cg_a:
+        c.wait_recv()
+    stores.append(pltpu.make_async_copy(ga.at[1 - gz], ga_h.at[1 - gz], esem.at[4]))
+    stores[4].start()
     for c in cg_d:
         c.wait_recv()
     stores.append(pltpu.make_async_copy(gd.at[1 - gz], gd_h.at[1 - gz], esem.at[5]))
-    stores[4].start()
-    for c in cg_a:
-        c.wait_recv()
-    stores.append(pltpu.make_async_copy(ga.at[1 - gz], ga_h.at[1 - gz], esem.at[4]))
     stores[5].start()
     for c in stores:
         c.wait()
@@ -461,34 +429,38 @@
             x_from(gd.at[gz, pl.ds(j * KD, KD)], xgsem, 1, j).wait_send()
 
         away(j, sent)
-    for c in (octs + cot_faces + rets + hid_faces + cores_a + cores_d + zs_a + zs_d + zg_a + cg_a + cg_d):
+    for c in (octs + cot_faces + rets + hid_faces + cores_a + cores_d + zs_a + zs_d + cg_a + cg_d):
         c.wait_send()
 
 
 def finish(coarse_h, fineg_h, ga_h, gd_h, coarse_o, fineg_o, down_h, conv_h,
            coarse, fineg, ga, gd, down, conv, sem):
-    reads = [pltpu.make_async_copy(src, dst, sem.at[i]) for i, (src, dst) in enumerate(
-        ((gd_h, gd), (ga_h, ga), (fineg_h, fineg), (coarse_h, coarse)))]
+    reads = [pltpu.make_async_copy(gd_h, gd, sem.at[0])]
+    for m in range(7):
+        rows = pl.ds(m * 256, 256)
+        reads.append(pltpu.make_async_copy(ga_h.at[:, rows], ga.at[:, rows], sem.at[1 + m]))
+    reads += [pltpu.make_async_copy(coarse_h, coarse, sem.at[8]), pltpu.make_async_copy(fineg_h, fineg, sem.at[9])]
     for c in reads:
         c.start()
-    writes = [pltpu.make_async_copy(src, dst, sem.at[4 + i]) for i, (src, dst) in enumerate(
-        ((down, down_h), (fineg, fineg_o), (coarse, coarse_o)))]
     scale = 1.0 / (64 * MB)
     reads[0].wait()
     for h in range(2):
         down[:, h * 128:(h + 1) * 128] = gd[h].astype(F32) * scale
+    writes = [pltpu.make_async_copy(down, down_h, sem.at[10])]
     writes[0].start()
-    reads[1].wait()
     for m in range(7):
+        reads[1 + m].wait()
         rows = slice(m * 256, (m + 1) * 256)
         for h in range(2):
             conv[rows, h * 128:(h + 1) * 128] = ga[h, rows].astype(F32) * scale
-        writes.append(pltpu.make_async_copy(conv.at[rows], conv_h.at[rows], sem.at[7 + m]))
-        writes[3 + m].start()
-    reads[2].wait()
-    writes[1].start()
-    reads[3].wait()
-    writes[2].start()
+        writes.append(pltpu.make_async_copy(conv.at[rows], conv_h.at[rows], sem.at[11 + m]))
+        writes[1 + m].start()
+    reads[8].wait()
+    writes.append(pltpu.make_async_copy(coarse, coarse_o, sem.at[18]))
+    writes[8].start()
+    reads[9].wait()
+    writes.append(pltpu.make_async_copy(fineg, fineg_o, sem.at[19]))
+    writes[9].start()
     for c in writes:
         c.wait()
 
@@ -549,10 +521,8 @@
             pltpu.VMEM((1024, 128), BF),
             pltpu.VMEM((NX, KA, 128), BF),
             pltpu.VMEM((NX, KD, 128), BF),
-            pltpu.VMEM((NY, 16, 128), BF),
-            pltpu.VMEM((NY, 16, 128), BF),
+            pltpu.VMEM((NY, KA, 128), BF),
             pltpu.VMEM((NY, KD, 128), BF),
-            pltpu.VMEM((NY, 16, 128), BF),
             dma((6,)),
             dma((6,)),
             dma((2, 8)),
@@ -561,7 +531,6 @@
             dma((2, 5)),
             dma((2, 11)),
             dma((2, 2 * NX)),
-            dma((2, 2 * NY)),
             dma((2, 2 * NY)),
             dma((2, 2 * NX)),
             dma((2, 8)),
@@ -589,7 +558,7 @@
             pltpu.VMEM((2, 1024, 128), BF),
             pltpu.VMEM((1024, 256), F32),
             pltpu.VMEM((1792, 256), F32),
-            dma((14,)),
+            dma((20,)),
         ],
         compiler_params=pltpu.CompilerParams(vmem_limit_bytes=60 * 1024 * 1024),
     )(coarse, fineg, ga, gd)

time: 64.6 us -> 63.9 us (0.989)
    pallas_call x1, Pallas kernels: 60.2 us -> 59.5 us  [shards(): pl.pallas_call(kernel, out_shape=(jax.ShapeDtypeStruct((16 * MB, 4, 256),...]
where the time goes in v5:
time: 63.9 us; the launch traced here: 63.8 us
  Pallas kernels  63 us (99%)
  between operations  0.8 us (1%)
    pallas_call x1, Pallas kernels, shards(): pl.pallas_call(kernel, out_shape=(jax.ShapeDtypeStruct((16 * MB, 4, 256),...  59.5 us
    pallas_call x1, Pallas kernels, shards(): pl.pallas_call(finish, out_shape=(jax.ShapeDtypeStruct((16 * MB, 4, 256),...  3.5 us

profile of v5, /device:TPU:1, one launch (start us, length us, event | category | flops | bytes accessed | tf_op | source)
XLA Modules:
  0.0 63.8 jit_solution(4839173230802199732)
XLA Ops:
  0.6 59.5 %shard_map.93 = (bf16[288,4,256]{2,1,0:T(4,128)(2,1)}, bf16[5120,128]{1,0:T(8,128)(2,1)}, bf16[2,1792,128]{2,1,0:T(8,128)(2,1)}, bf16[2,1024,128]{2,1,0:T(8,128)(2,1)}) custom-call(bf16[5120,128]{1,0:T(8,128)(2,1)} %bitcast.9, s32[1,80]{1,0:T(1,128)} %bitcast.15, s32[6,18]{1,0:T(8,128)} %bitcast.14, bf16[1024,256]{1,0:T(8,128)(2,1)} %wd_h.1, ...), custom_call_target="tpu_custom_call" | custom-call | flops 6000000000 | bytes 10000000 | tf_op jit(solution)/shard_map/pallas_call | solution.py:471
  60.2 3.5 %shard_map.94 = (bf16[288,4,256]{2,1,0:T(4,128)(2,1)}, bf16[5120,128]{1,0:T(8,128)(2,1)}, f32[1024,256]{1,0:T(8,128)}, f32[1792,256]{1,0:T(8,128)}) custom-call(bf16[288,4,256]{2,1,0:T(4,128)(2,1)} %get-tuple-element.12.coarse_h, bf16[5120,128]{1,0:T(8,128)(2,1)} %get-tuple-element.13.fineg_h, bf16[2,1792,128]{2,1,0:T(8,128)(2,1)} %get-tuple-element.14.ga_h, ...), custom_call_target="tpu_custom_call" | custom-call | tf_op jit(solution)/shard_map/pallas_call | solution.py:544

commit v6 on v5

--- a/solution.py
+++ b/solution.py
@@ -99,7 +99,7 @@
         pl.semaphore_signal(barrier, inc=1, device_id=peer, device_id_type=MESH)
 
     loads = [pltpu.make_async_copy(src, dst, isem.at[i]) for i, (src, dst) in enumerate(
-        ((cot_h, cin), (fine_h, fin), (wd_h, wd), (wc_h, wc), (nb_h, nb), (tgt_h, tgt)))]
+        ((tgt_h, tgt), (fine_h, fin), (wd_h, wd), (cot_h, cin), (nb_h, nb), (wc_h, wc)))]
     for c in loads:
         c.start()
 
@@ -107,71 +107,6 @@
         return pltpu.make_async_remote_copy(
             src_ref=src, dst_ref=dst, send_sem=sems.at[0, i], recv_sem=sems.at[1, i],
             device_id=device, device_id_type=MESH)
-
-    quad_c = lax.shift_right_arithmetic(iota((128, 128), 0), 5)
-    lane = iota((128, 128), 1)
-
-    loads[4].wait()
-    n_scr[...] = jnp.full((8, 128), -1, I32)
-    for q in range(4):
-        n_scr[0:6, BP * q:BP * q + MB] = nb[...]
-    nb_r = n_scr[...]
-    nb_c = nb_r.T
-
-    def names(v):
-        owner = ninth(lax.shift_right_arithmetic(v, 1))
-        return v - owner * MB, (v >= 0) & (owner == myself), (v >= 0) & (owner != myself)
-
-    for k in range(6):
-        vc = nb_c[:, k:k + 1]
-        vr = nb_r[k:k + 1, :]
-        idx_c, home_c, far_c = names(vc)
-        idx_r, home_r, far_r = names(vr)
-        less = far_r & (vr < vc) & (lane < 32)
-        rank_c = jnp.sum(jnp.where(less, 1.0, 0.0), axis=1, keepdims=True).astype(I32)
-        selp[k, :, 0:128] = onehot(home_c & (idx_c + 32 * quad_c == lane))
-        selp[k, :, 128:256] = onehot(far_c & (rank_c + 8 * quad_c == lane))
-        early = far_c[0:32] & (iota((32, 128), 0) < (iota((32, 128), 1) & 31))
-        rank_r = jnp.sum(jnp.where(early, 1.0, 0.0), axis=0, keepdims=True).astype(I32)
-        slot = rank_r + 8 * lax.shift_right_arithmetic(iota((32, 128), 1), 5)
-        selc[k] = onehot(far_r & (slot == iota((32, 128), 0)))
-
-    face_to = (at(1, 0), at(-1, 0), at(0, 1), at(0, -1), other)
-
-    def send_faces(ext, snd, rcv, sems):
-        copies = [remote(snd.at[k], rcv.at[k], sems, k, face_to[k]) for k in range(5)]
-        for k in range(4):
-            for q in range(4):
-                snd[k, q * 32:(q + 1) * 32, :] = dot(selc[OPP[k + 1] - 1], layer_quad(ext, k, q)).astype(BF)
-            copies[k].start()
-        for q in range(4):
-            both = dot(selc[5], layer_quad(ext, 4, q)) + dot(selc[4], layer_quad(ext, 5, q))
-            snd[4, q * 32:(q + 1) * 32, :] = both.astype(BF)
-        copies[4].start()
-        return copies
-
-    def take_faces(ext, rcv, copies):
-        for c in copies:
-            c.wait_recv()
-        for k in range(6):
-            for q in range(4):
-                near = dot(selp[k, :, 0:128], layer_quad(ext, k, q))
-                far = dot(selp[k, :, 128:160], rcv[min(k, 4), q * 32:(q + 1) * 32, :])
-                put_halo(ext, k, q, (near + far).astype(BF))
-
-    loads[0].wait()
-    tall[...] = jnp.zeros_like(tall)
-    for m in range(16 * MB):
-        part = cin[m].astype(F32)
-        for h in range(2):
-            tall[h, 4 * m:4 * m + 4, :] = part[:, h * 128:(h + 1) * 128]
-    for p in range(64):
-        x, y, z = p >> 4, (p >> 2) & 3, p & 3
-        for h in range(2):
-            rows = tall[h, pl.ds(p, BP, stride=64), :]
-            cotx[1 + x, 1 + y, BP * (1 + z):BP * (2 + z), h * 128:(h + 1) * 128] = rows.astype(BF)
-    pl.semaphore_wait(barrier, len(peers))
-    cot_faces = send_faces(cotx, fsnd, frcv, fsem)
 
     def place(t):
         owner = ninth(lax.shift_right_arithmetic(t, 4))
@@ -182,7 +117,7 @@
         flat = (sx + 1) * 3 + (sy + 1)
         return cell, moving, jnp.where(flat > 4, flat - 1, flat)
 
-    loads[5].wait()
+    loads[0].wait()
     t_scr[:, 0:NB] = jnp.broadcast_to(tgt[...], (128, NB))
     cell_c, moving_c, dest_c = place(t_scr[...].T[0:NB, 0:1])
     cell_r, moving_r, dest_r = place(tgt[...])
@@ -223,23 +158,82 @@
     for d in range(8):
         osnd[d, 64:80, :] = out[d * 16:(d + 1) * 16]
 
+    pl.semaphore_wait(barrier, len(peers))
     octs = [remote(osnd.at[d], orcv.at[d], osem, d, at(*DIRS[d])) for d in range(8)]
     for c in octs:
         c.start()
+
+    quad_c = lax.shift_right_arithmetic(iota((128, 128), 0), 5)
+    lane = iota((128, 128), 1)
+
+    loads[4].wait()
+    n_scr[...] = jnp.full((8, 128), -1, I32)
+    for q in range(4):
+        n_scr[0:6, BP * q:BP * q + MB] = nb[...]
+    nb_r = n_scr[...]
+    nb_c = nb_r.T
+
+    def names(v):
+        owner = ninth(lax.shift_right_arithmetic(v, 1))
+        return v - owner * MB, (v >= 0) & (owner == myself), (v >= 0) & (owner != myself)
+
+    for k in range(6):
+        vc = nb_c[:, k:k + 1]
+        vr = nb_r[k:k + 1, :]
+        idx_c, home_c, far_c = names(vc)
+        idx_r, home_r, far_r = names(vr)
+        less = far_r & (vr < vc) & (lane < 32)
+        rank_c = jnp.sum(jnp.where(less, 1.0, 0.0), axis=1, keepdims=True).astype(I32)
+        selp[k, :, 0:128] = onehot(home_c & (idx_c + 32 * quad_c == lane))
+        selp[k, :, 128:256] = onehot(far_c & (rank_c + 8 * quad_c == lane))
+        early = far_c[0:32] & (iota((32, 128), 0) < (iota((32, 128), 1) & 31))
+        rank_r = jnp.sum(jnp.where(early, 1.0, 0.0), axis=0, keepdims=True).astype(I32)
+        slot = rank_r + 8 * lax.shift_right_arithmetic(iota((32, 128), 1), 5)
+        selc[k] = onehot(far_r & (slot == iota((32, 128), 0)))
+
+    face_to = (at(1, 0), at(-1, 0), at(0, 1), at(0, -1), other)
+
+    def send_faces(ext, snd, rcv, sems):
+        copies = [remote(snd.at[k], rcv.at[k], sems, k, face_to[k]) for k in range(5)]
+        for k in range(4):
+            for q in range(4):
+                snd[k, q * 32:(q + 1) * 32, :] = dot(selc[OPP[k + 1] - 1], layer_quad(ext, k, q)).astype(BF)
+            copies[k].start()
+        for q in range(4):
+            both = dot(selc[5], layer_quad(ext, 4, q)) + dot(selc[4], layer_quad(ext, 5, q))
+            snd[4, q * 32:(q + 1) * 32, :] = both.astype(BF)
+        copies[4].start()
+        return copies
+
+    def take_faces(ext, rcv, copies):
+        for c in copies:
+            c.wait_recv()
+        for k in range(6):
+            for q in range(4):
+                near = dot(selp[k, :, 0:128], layer_quad(ext, k, q))
+                far = dot(selp[k, :, 128:160], rcv[min(k, 4), q * 32:(q + 1) * 32, :])
+                put_halo(ext, k, q, (near + far).astype(BF))
+
+    loads[3].wait()
+    tall[...] = jnp.zeros_like(tall)
+    for m in range(16 * MB):
+        part = cin[m].astype(F32)
+        for h in range(2):
+            tall[h, 4 * m:4 * m + 4, :] = part[:, h * 128:(h + 1) * 128]
+    for p in range(64):
+        x, y, z = p >> 4, (p >> 2) & 3, p & 3
+        for h in range(2):
+            rows = tall[h, pl.ds(p, BP, stride=64), :]
+            cotx[1 + x, 1 + y, BP * (1 + z):BP * (2 + z), h * 128:(h + 1) * 128] = rows.astype(BF)
+    cot_faces = send_faces(cotx, fsnd, frcv, fsem)
 
     fine_t[...] = fine[...].T
     pre = red[...].astype(F32)
     sig = 1.0 / (1.0 + jnp.exp(-pre))
     slope[...] = sig * (1.0 + pre * (1.0 - sig))
-    loads[3].wait()
+    loads[5].wait()
     for d in range(7):
         wt[d * 256:(d + 1) * 256, :] = wc[d * 256:(d + 1) * 256, :].T
-    take_faces(cotx, frcv, cot_faces)
-
-    for x in range(4):
-        rows = jnp.concatenate([view(cotx, x, OPP[d]) for d in range(7)], axis=1)
-        gh[x] = dot(rows, wt[...]).astype(BF)
-
     for c in octs:
         c.wait_recv()
     tag = orcv[:, 64:80, :].reshape(128, 256).astype(F32)
@@ -248,22 +242,6 @@
     came = [jnp.where(match & (row_half == h), 1.0, 0.0) for h in range(2)]
     came_t = [m.T.astype(BF) for m in came]
     came = [m.astype(BF) for m in came]
-
-    def grads(c):
-        i, j, k = c >> 2, (c >> 1) & 1, c & 1
-        out = []
-        for o in range(8):
-            x, y, z = 2 * (o >> 2) + i, 2 * ((o >> 1) & 1) + j, 2 * (o & 1) + k
-            out.append(gh[x, (y * 4 + z) * BP:(y * 4 + z + 1) * BP, :])
-        return jnp.concatenate(out, axis=0)
-
-    for pair in range(4):
-        out = (dot(came[0], grads(2 * pair)) + dot(came[1], grads(2 * pair + 1))).astype(BF)
-        for d in range(8):
-            rsnd[d, pair * 16:(pair + 1) * 16, :] = out[d * 16:(d + 1) * 16]
-    rets = [remote(rsnd.at[d], rrcv.at[d], rsem, d, at(-DIRS[d][0], -DIRS[d][1])) for d in range(8)]
-    for c in rets:
-        c.start()
 
     for c in range(8):
         i, j, k = c >> 2, (c >> 1) & 1, c & 1
@@ -275,6 +253,30 @@
             x, y, z = 2 * (o >> 2) + i, 2 * ((o >> 1) & 1) + j, 2 * (o & 1) + k
             hidx[1 + x, 1 + y, BP * (1 + z):BP * (2 + z), :] = hid[o * BP:(o + 1) * BP]
     hid_faces = send_faces(hidx, hsnd, hrcv, hsem)
+    for x in range(4):
+        hid_t[:, x * 512:(x + 1) * 512] = view(hidx, x, 0).T
+
+    take_faces(cotx, frcv, cot_faces)
+
+    for x in range(4):
+        rows = jnp.concatenate([view(cotx, x, OPP[d]) for d in range(7)], axis=1)
+        gh[x] = dot(rows, wt[...]).astype(BF)
+
+    def grads(c):
+        i, j, k = c >> 2, (c >> 1) & 1, c & 1
+        out = []
+        for o in range(8):
+            x, y, z = 2 * (o >> 2) + i, 2 * ((o >> 1) & 1) + j, 2 * (o & 1) + k
+            out.append(gh[x, (y * 4 + z) * BP:(y * 4 + z + 1) * BP, :])
+        return jnp.concatenate(out, axis=0)
+
+    for pair in range(4):
+        out = (dot(came[0], grads(2 * pair)) + dot(came[1], grads(2 * pair + 1))).astype(BF)
+        for d in range(8):
+            rsnd[d, pair * 16:(pair + 1) * 16, :] = out[d * 16:(d + 1) * 16]
+    rets = [remote(rsnd.at[d], rrcv.at[d], rsem, d, at(-DIRS[d][0], -DIRS[d][1])) for d in range(8)]
+    for c in rets:
+        c.start()
 
     def core_send(p, cbuf, m, s):
         rows = pl.ds(m * 256, 256)
@@ -345,8 +347,6 @@
             out[quarter].start()
         return out
 
-    for x in range(4):
-        hid_t[:, x * 512:(x + 1) * 512] = view(hidx, x, 0).T
     cores_a = []
     for d in range(7):
         rows = jnp.concatenate([view(cotx, x, OPP[d]) for x in range(4)], axis=0)

time: 63.9 us -> 64.1 us (level)
  no operation moved by 1% of the time
where the time goes in v6:
time: 64.1 us; the launch traced here: 64 us
  Pallas kernels  63.2 us (99%)
  between operations  0.8 us (1%)
    pallas_call x1, Pallas kernels, shards(): pl.pallas_call(kernel, out_shape=(jax.ShapeDtypeStruct((16 * MB, 4, 256),...  59.7 us
    pallas_call x1, Pallas kernels, shards(): pl.pallas_call(finish, out_shape=(jax.ShapeDtypeStruct((16 * MB, 4, 256),...  3.5 us

profile of v6, /device:TPU:1, one launch (start us, length us, event | category | flops | bytes accessed | tf_op | source)
XLA Modules:
  0.0 64.0 jit_solution(7455790031206219411)
XLA Ops:
  0.6 59.7 %shard_map.93 = (bf16[288,4,256]{2,1,0:T(4,128)(2,1)}, bf16[5120,128]{1,0:T(8,128)(2,1)}, bf16[2,1792,128]{2,1,0:T(8,128)(2,1)}, bf16[2,1024,128]{2,1,0:T(8,128)(2,1)}) custom-call(bf16[5120,128]{1,0:T(8,128)(2,1)} %bitcast.9, s32[1,80]{1,0:T(1,128)} %bitcast.15, s32[6,18]{1,0:T(8,128)} %bitcast.14, bf16[1024,256]{1,0:T(8,128)(2,1)} %wd_h.1, ...), custom_call_target="tpu_custom_call" | custom-call | flops 6000000000 | bytes 10000000 | tf_op jit(solution)/shard_map/pallas_call | solution.py:471
  60.4 3.5 %shard_map.94 = (bf16[288,4,256]{2,1,0:T(4,128)(2,1)}, bf16[5120,128]{1,0:T(8,128)(2,1)}, f32[1024,256]{1,0:T(8,128)}, f32[1792,256]{1,0:T(8,128)}) custom-call(bf16[288,4,256]{2,1,0:T(4,128)(2,1)} %get-tuple-element.12.coarse_h, bf16[5120,128]{1,0:T(8,128)(2,1)} %get-tuple-element.13.fineg_h, bf16[2,1792,128]{2,1,0:T(8,128)(2,1)} %get-tuple-element.14.ga_h, ...), custom_call_target="tpu_custom_call" | custom-call | tf_op jit(solution)/shard_map/pallas_call | solution.py:544

commit v7 on v6

--- a/solution.py
+++ b/solution.py
@@ -81,9 +81,9 @@
            coarse_h, fineg_h, ga_h, gd_h,
            tgt, nb, ga, gd, fin, cin, wd, wc, wt, t_scr, n_scr, wide, tall, fine, coarse_v, fineg_v,
            cotx, hidx, gh, red, slope, fine_t, hid_t, gr, selc, selp,
-           osnd, orcv, rsnd, rrcv, fsnd, frcv, hsnd, hrcv,
+           nsnd, nrcv, osnd, orcv, rsnd, rrcv, fsnd, frcv, hsnd, hrcv,
            pa, pd, ca, cd, qa, qd, xa, xd, ya, yd,
-           isem, esem, osem, rsem, fsem, hsem, coresem, xsem, zsem, xgsem, cgsem):
+           isem, esem, nsem, osem, rsem, fsem, hsem, coresem, xsem, zsem, xgsem, cgsem):
     gx, gy, gz = lax.axis_index("gx"), lax.axis_index("gy"), lax.axis_index("gz")
     myself = (gx * NY + gy) * NZ + gz
 
@@ -99,7 +99,7 @@
         pl.semaphore_signal(barrier, inc=1, device_id=peer, device_id_type=MESH)
 
     loads = [pltpu.make_async_copy(src, dst, isem.at[i]) for i, (src, dst) in enumerate(
-        ((tgt_h, tgt), (fine_h, fin), (wd_h, wd), (cot_h, cin), (nb_h, nb), (wc_h, wc)))]
+        ((tgt_h, tgt), (cot_h, cin), (nb_h, nb), (fine_h, fin), (wd_h, wd), (wc_h, wc)))]
     for c in loads:
         c.start()
 
@@ -140,33 +140,15 @@
     stay_c = onehot((cell_c == table_name((NB, 256), 1)) & jnp.logical_not(moving_c))
     stay_r = onehot((cell_r == table_name((256, NB), 0)) & jnp.logical_not(moving_r))
 
-    loads[1].wait()
-    wide[...] = fin[...].astype(F32)
-    for c in range(8):
-        for v in range(8):
-            part = wide[pl.ds(c * 8 + v, NB, stride=64), :]
-            fine[c * NB:(c + 1) * NB, v * 128:(v + 1) * 128] = part.astype(BF)
-    loads[2].wait()
-    red[...] = dot(fine[...], wd[...]).astype(BF)
-    for pair in range(4):
-        out = sum(dot(send_hot[h], red[(2 * pair + h) * NB:(2 * pair + h + 1) * NB, :]) for h in range(2))
-        out = out.astype(BF)
-        for d in range(8):
-            osnd[d, pair * 16:(pair + 1) * 16, :] = out[d * 16:(d + 1) * 16]
     tags = jnp.broadcast_to((cell_c + 1).astype(F32), (NB, 256)).astype(BF)
     out = (dot(send_hot[0], tags) + dot(send_hot[1], tags)).astype(BF)
     for d in range(8):
-        osnd[d, 64:80, :] = out[d * 16:(d + 1) * 16]
-
-    pl.semaphore_wait(barrier, len(peers))
-    octs = [remote(osnd.at[d], orcv.at[d], osem, d, at(*DIRS[d])) for d in range(8)]
-    for c in octs:
-        c.start()
+        nsnd[d] = out[d * 16:(d + 1) * 16]
 
     quad_c = lax.shift_right_arithmetic(iota((128, 128), 0), 5)
     lane = iota((128, 128), 1)
 
-    loads[4].wait()
+    loads[2].wait()
     n_scr[...] = jnp.full((8, 128), -1, I32)
     for q in range(4):
         n_scr[0:6, BP * q:BP * q + MB] = nb[...]
@@ -214,7 +196,7 @@
                 far = dot(selp[k, :, 128:160], rcv[min(k, 4), q * 32:(q + 1) * 32, :])
                 put_halo(ext, k, q, (near + far).astype(BF))
 
-    loads[3].wait()
+    loads[1].wait()
     tall[...] = jnp.zeros_like(tall)
     for m in range(16 * MB):
         part = cin[m].astype(F32)
@@ -225,7 +207,28 @@
         for h in range(2):
             rows = tall[h, pl.ds(p, BP, stride=64), :]
             cotx[1 + x, 1 + y, BP * (1 + z):BP * (2 + z), h * 128:(h + 1) * 128] = rows.astype(BF)
+    pl.semaphore_wait(barrier, len(peers))
+    tells = [remote(nsnd.at[d], nrcv.at[d], nsem, d, at(*DIRS[d])) for d in range(8)]
+    for c in tells:
+        c.start()
     cot_faces = send_faces(cotx, fsnd, frcv, fsem)
+
+    loads[3].wait()
+    wide[...] = fin[...].astype(F32)
+    for c in range(8):
+        for v in range(8):
+            part = wide[pl.ds(c * 8 + v, NB, stride=64), :]
+            fine[c * NB:(c + 1) * NB, v * 128:(v + 1) * 128] = part.astype(BF)
+    loads[4].wait()
+    red[...] = dot(fine[...], wd[...]).astype(BF)
+    for pair in range(4):
+        out = sum(dot(send_hot[h], red[(2 * pair + h) * NB:(2 * pair + h + 1) * NB, :]) for h in range(2))
+        out = out.astype(BF)
+        for d in range(8):
+            osnd[d, pair * 16:(pair + 1) * 16, :] = out[d * 16:(d + 1) * 16]
+    octs = [remote(osnd.at[d], orcv.at[d], osem, d, at(*DIRS[d])) for d in range(8)]
+    for c in octs:
+        c.start()
 
     fine_t[...] = fine[...].T
     pre = red[...].astype(F32)
@@ -234,15 +237,39 @@
     loads[5].wait()
     for d in range(7):
         wt[d * 256:(d + 1) * 256, :] = wc[d * 256:(d + 1) * 256, :].T
-    for c in octs:
+    take_faces(cotx, frcv, cot_faces)
+
+    for x in range(4):
+        rows = jnp.concatenate([view(cotx, x, OPP[d]) for d in range(7)], axis=1)
+        gh[x] = dot(rows, wt[...]).astype(BF)
+
+    for c in tells:
         c.wait_recv()
-    tag = orcv[:, 64:80, :].reshape(128, 256).astype(F32)
+    tag = nrcv[...].reshape(128, 256).astype(F32)
     row_half = lax.shift_right_arithmetic(iota((128, 256), 0), 3) & 1
     match = tag - 1.0 == table_name((128, 256), 1).astype(F32)
     came = [jnp.where(match & (row_half == h), 1.0, 0.0) for h in range(2)]
     came_t = [m.T.astype(BF) for m in came]
     came = [m.astype(BF) for m in came]
 
+    def grads(c):
+        i, j, k = c >> 2, (c >> 1) & 1, c & 1
+        out = []
+        for o in range(8):
+            x, y, z = 2 * (o >> 2) + i, 2 * ((o >> 1) & 1) + j, 2 * (o & 1) + k
+            out.append(gh[x, (y * 4 + z) * BP:(y * 4 + z + 1) * BP, :])
+        return jnp.concatenate(out, axis=0)
+
+    for pair in range(4):
+        out = (dot(came[0], grads(2 * pair)) + dot(came[1], grads(2 * pair + 1))).astype(BF)
+        for d in range(8):
+            rsnd[d, pair * 16:(pair + 1) * 16, :] = out[d * 16:(d + 1) * 16]
+    rets = [remote(rsnd.at[d], rrcv.at[d], rsem, d, at(-DIRS[d][0], -DIRS[d][1])) for d in range(8)]
+    for c in rets:
+        c.start()
+
+    for c in octs:
+        c.wait_recv()
     for c in range(8):
         i, j, k = c >> 2, (c >> 1) & 1, c & 1
         pair = c >> 1
@@ -253,30 +280,6 @@
             x, y, z = 2 * (o >> 2) + i, 2 * ((o >> 1) & 1) + j, 2 * (o & 1) + k
             hidx[1 + x, 1 + y, BP * (1 + z):BP * (2 + z), :] = hid[o * BP:(o + 1) * BP]
     hid_faces = send_faces(hidx, hsnd, hrcv, hsem)
-    for x in range(4):
-        hid_t[:, x * 512:(x + 1) * 512] = view(hidx, x, 0).T
-
-    take_faces(cotx, frcv, cot_faces)
-
-    for x in range(4):
-        rows = jnp.concatenate([view(cotx, x, OPP[d]) for d in range(7)], axis=1)
-        gh[x] = dot(rows, wt[...]).astype(BF)
-
-    def grads(c):
-        i, j, k = c >> 2, (c >> 1) & 1, c & 1
-        out = []
-        for o in range(8):
-            x, y, z = 2 * (o >> 2) + i, 2 * ((o >> 1) & 1) + j, 2 * (o & 1) + k
-            out.append(gh[x, (y * 4 + z) * BP:(y * 4 + z + 1) * BP, :])
-        return jnp.concatenate(out, axis=0)
-
-    for pair in range(4):
-        out = (dot(came[0], grads(2 * pair)) + dot(came[1], grads(2 * pair + 1))).astype(BF)
-        for d in range(8):
-            rsnd[d, pair * 16:(pair + 1) * 16, :] = out[d * 16:(d + 1) * 16]
-    rets = [remote(rsnd.at[d], rrcv.at[d], rsem, d, at(-DIRS[d][0], -DIRS[d][1])) for d in range(8)]
-    for c in rets:
-        c.start()
 
     def core_send(p, cbuf, m, s):
         rows = pl.ds(m * 256, 256)
@@ -347,6 +350,8 @@
             out[quarter].start()
         return out
 
+    for x in range(4):
+        hid_t[:, x * 512:(x + 1) * 512] = view(hidx, x, 0).T
     cores_a = []
     for d in range(7):
         rows = jnp.concatenate([view(cotx, x, OPP[d]) for x in range(4)], axis=0)
@@ -429,7 +434,7 @@
             x_from(gd.at[gz, pl.ds(j * KD, KD)], xgsem, 1, j).wait_send()
 
         away(j, sent)
-    for c in (octs + cot_faces + rets + hid_faces + cores_a + cores_d + zs_a + zs_d + cg_a + cg_d):
+    for c in (tells + octs + cot_faces + rets + hid_faces + cores_a + cores_d + zs_a + zs_d + cg_a + cg_d):
         c.wait_send()
 
 
@@ -505,8 +510,10 @@
             pltpu.VMEM((8 * NB, 256), BF),
             pltpu.VMEM((6, 32, 128), BF),
             pltpu.VMEM((6, 128, 256), BF),
-            pltpu.VMEM((8, 80, 256), BF),
-            pltpu.VMEM((8, 80, 256), BF),
+            pltpu.VMEM((8, 16, 256), BF),
+            pltpu.VMEM((8, 16, 256), BF),
+            pltpu.VMEM((8, 64, 256), BF),
+            pltpu.VMEM((8, 64, 256), BF),
             pltpu.VMEM((8, 64, 256), BF),
             pltpu.VMEM((8, 64, 256), BF),
             pltpu.VMEM((5, 128, 256), BF),
@@ -525,6 +532,7 @@
             pltpu.VMEM((NY, KD, 128), BF),
             dma((6,)),
             dma((6,)),
+            dma((2, 8)),
             dma((2, 8)),
             dma((2, 8)),
             dma((2, 5)),

time: 64.1 us -> 63.3 us (0.988)
  Pallas kernels: 63.2 us -> 62.4 us
    pallas_call x1, Pallas kernels: 59.7 us -> 58.9 us  [shards(): pl.pallas_call(kernel, out_shape=(jax.ShapeDtypeStruct((16 * MB, 4, 256),...]
where the time goes in v7:
time: 63.3 us; the launch traced here: 63.2 us
  Pallas kernels  62.4 us (99%)
  between operations  0.8 us (1%)
    pallas_call x1, Pallas kernels, shards(): pl.pallas_call(kernel, out_shape=(jax.ShapeDtypeStruct((16 * MB, 4, 256),...  58.9 us
    pallas_call x1, Pallas kernels, shards(): pl.pallas_call(finish, out_shape=(jax.ShapeDtypeStruct((16 * MB, 4, 256),...  3.5 us

profile of v7, /device:TPU:1, one launch (start us, length us, event | category | flops | bytes accessed | tf_op | source)
XLA Modules:
  0.0 63.2 jit_solution(1551724386775113091)
XLA Ops:
  0.6 58.9 %shard_map.93 = (bf16[288,4,256]{2,1,0:T(4,128)(2,1)}, bf16[5120,128]{1,0:T(8,128)(2,1)}, bf16[2,1792,128]{2,1,0:T(8,128)(2,1)}, bf16[2,1024,128]{2,1,0:T(8,128)(2,1)}) custom-call(bf16[5120,128]{1,0:T(8,128)(2,1)} %bitcast.9, s32[1,80]{1,0:T(1,128)} %bitcast.15, s32[6,18]{1,0:T(8,128)} %bitcast.14, bf16[1024,256]{1,0:T(8,128)(2,1)} %wd_h.1, ...), custom_call_target="tpu_custom_call" | custom-call | flops 6000000000 | bytes 10000000 | tf_op jit(solution)/shard_map/pallas_call | solution.py:476
  59.5 3.5 %shard_map.94 = (bf16[288,4,256]{2,1,0:T(4,128)(2,1)}, bf16[5120,128]{1,0:T(8,128)(2,1)}, f32[1024,256]{1,0:T(8,128)}, f32[1792,256]{1,0:T(8,128)}) custom-call(bf16[288,4,256]{2,1,0:T(4,128)(2,1)} %get-tuple-element.12.coarse_h, bf16[5120,128]{1,0:T(8,128)(2,1)} %get-tuple-element.13.fineg_h, bf16[2,1792,128]{2,1,0:T(8,128)(2,1)} %get-tuple-element.14.ga_h, ...), custom_call_target="tpu_custom_call" | custom-call | tf_op jit(solution)/shard_map/pallas_call | solution.py:552

commit v8 on v7

--- a/solution.py
+++ b/solution.py
@@ -377,9 +377,9 @@
             pd[h, m * 256:(m + 1) * 256, :] = acc[:, h * 128:(h + 1) * 128]
         cores_d.append(core_send(pd, cd, m, 1))
 
-    take_faces(hidx, hrcv, hid_faces)
     for m in range(4):
         core_take(cores_d[m], pd, cd, qd, xd, KD, m, 1)
+    take_faces(hidx, hrcv, hid_faces)
 
     def conv(x):
         rows = jnp.concatenate([view(hidx, x, d) for d in range(7)], axis=1)
@@ -388,10 +388,9 @@
             for h in range(2):
                 tall[h, pl.ds(x * 16 + p, BP, stride=64), :] = acc[p * BP:(p + 1) * BP, h * 128:(h + 1) * 128]
 
-    for x in range(3):
+    for x in range(4):
         conv(x)
     zs_a = zb_start(x_sum(qa, xa, KA, 0), ya, 0)
-    conv(3)
     zs_d = zb_start(x_sum(qd, xd, KD, 1), yd, 1)
 
     for c in range(8):

time: 63.3 us -> 63.8 us (level)
  no operation moved by 1% of the time
where the time goes in v8:
time: 63.8 us; the launch traced here: 63.7 us
  Pallas kernels  62.9 us (99%)
  between operations  0.8 us (1%)
    pallas_call x1, Pallas kernels, shards(): pl.pallas_call(kernel, out_shape=(jax.ShapeDtypeStruct((16 * MB, 4, 256),...  59.5 us
    pallas_call x1, Pallas kernels, shards(): pl.pallas_call(finish, out_shape=(jax.ShapeDtypeStruct((16 * MB, 4, 256),...  3.5 us

profile of v8, /device:TPU:1, one launch (start us, length us, event | category | flops | bytes accessed | tf_op | source)
XLA Modules:
  0.0 63.7 jit_solution(9495734452263515213)
XLA Ops:
  0.6 59.5 %shard_map.93 = (bf16[288,4,256]{2,1,0:T(4,128)(2,1)}, bf16[5120,128]{1,0:T(8,128)(2,1)}, bf16[2,1792,128]{2,1,0:T(8,128)(2,1)}, bf16[2,1024,128]{2,1,0:T(8,128)(2,1)}) custom-call(bf16[5120,128]{1,0:T(8,128)(2,1)} %bitcast.9, s32[1,80]{1,0:T(1,128)} %bitcast.15, s32[6,18]{1,0:T(8,128)} %bitcast.14, bf16[1024,256]{1,0:T(8,128)(2,1)} %wd_h.1, ...), custom_call_target="tpu_custom_call" | custom-call | flops 6000000000 | bytes 10000000 | tf_op jit(solution)/shard_map/pallas_call | solution.py:475
  60.1 3.5 %shard_map.94 = (bf16[288,4,256]{2,1,0:T(4,128)(2,1)}, bf16[5120,128]{1,0:T(8,128)(2,1)}, f32[1024,256]{1,0:T(8,128)}, f32[1792,256]{1,0:T(8,128)}) custom-call(bf16[288,4,256]{2,1,0:T(4,128)(2,1)} %get-tuple-element.12.coarse_h, bf16[5120,128]{1,0:T(8,128)(2,1)} %get-tuple-element.13.fineg_h, bf16[2,1792,128]{2,1,0:T(8,128)(2,1)} %get-tuple-element.14.ga_h, ...), custom_call_target="tpu_custom_call" | custom-call | tf_op jit(solution)/shard_map/pallas_call | solution.py:551
